TPU v7x, 32 devices: a whole 2x2x4 slice. The times are simulated.
32 devices in a mesh: seq: 8 (over z, x), head: 4 (over y, core).
Axes of the slice: x: 2, y: 2, z: 4, core: 2. Of those that a mesh axis runs over, the one named last changes fastest.
Arguments:
- inputs: float32 [8192, 4096], P('seq', 'head'), may hold values from -6 to 6
- cotangent: float32 [8192, 4096], P('seq', 'head'), may hold values from -1.5 to 1.5
- b_proj: float32 [8192, 128], P('seq'), may hold values from -1.8 to 1.8
- c_proj: float32 [8192, 128], P('seq'), may hold values from -1.8 to 1.8
- decay_rate: float32 [64], P('head'), may hold values from 1e-06 to 0.0001
- level_weight: float32 [8, 64, 8192], P(None, 'head', 'seq'), may hold values from 0 to 2, as said below
- starts: int32 [128], P('seq'), may hold values from 0 to 1, as said below
Outputs:
- grad_x: float32 [8192, 4096], P('seq', 'head')
- grad_b: float32 [8192, 128], P(('seq', 'head'))
- grad_c: float32 [8192, 128], P(('seq', 'head'))
- grad_level: float32 [8, 64, 8192], P(None, 'head', 'seq')
Inputs may be any that keep to these rules, and one draw needn't show every extreme that they name: `starts`: exactly two of the 128 stretches carry 1. `level_weight`: positive.
All inputs are finite; a program needn't handle non-finite values.
Results may differ from a plain program's by a relative error of at most 0.0001.
Values sent between devices are 32-bit elements; how exact they have to be, the bound alone decides.
No kernel may reach another device: no remote copies, remote signals or barrier semaphores. Data moves between devices by JAX's collectives and lax.ppermute only.
A program may use at most 128 MiB of HBM per device.

v0:
```python
import jax
import jax.numpy as jnp
from jax import lax
from jax.sharding import PartitionSpec as P

STRETCH = 64


def from_partner(x, axis, apart):
    return lax.ppermute(x, axis, [(i, i ^ 1 << apart) for i in range(lax.axis_size(axis))])


def local(inputs, cotangent, b_proj, c_proj, decay_rate, level_weight, starts):
    highest = lax.Precision.HIGHEST
    rows_dev = inputs.shape[0]
    head_count = decay_rate.shape[0]
    width = inputs.shape[1] // head_count
    seq_count = lax.axis_size("seq")
    seq_bits = seq_count.bit_length() - 1
    stretch_count = rows_dev // STRETCH
    stretch_bits = stretch_count.bit_length() - 1
    seq_index = lax.axis_index("seq")
    level_count = level_weight.shape[0]
    level_scale = (STRETCH * 2.0 ** jnp.arange(level_count, dtype=jnp.float32)) ** (-0.5)
    level_vals = level_weight * level_scale[:, None, None]
    position = (seq_index * rows_dev + jnp.arange(rows_dev) - seq_count * rows_dev // 2).astype(
        jnp.float32
    )
    decay_query = jnp.exp(-decay_rate[:, None] * position[None, :])
    decay_key = jnp.exp(decay_rate[:, None] * position[None, :])
    open_flag = 1.0 - starts.astype(jnp.float32)
    prefix_open = jnp.cumprod(open_flag)
    suffix_open = jnp.concatenate(
        [jnp.cumprod(open_flag[::-1])[::-1][1:], jnp.ones((1,), jnp.float32)]
    )
    device_clean = prefix_open[stretch_count - 1]
    prefix_rows = jnp.repeat(prefix_open, STRETCH)
    suffix_rows = jnp.repeat(suffix_open, STRETCH)
    x_heads = inputs.reshape(rows_dev, head_count, width)
    cot_heads = cotangent.reshape(rows_dev, head_count, width)
    key_weight = decay_key * suffix_rows[None, :]
    tail_total = jnp.einsum(
        "sn,shp->hnp", b_proj, x_heads * key_weight.T[:, :, None], precision=highest
    )
    query_weight = decay_query * prefix_rows[None, :]
    cross_level = level_vals[stretch_bits + 1 :]
    head_totals = jnp.einsum(
        "tn,kthp->khnp",
        c_proj,
        cot_heads[None] * jnp.transpose(cross_level * query_weight[None], (0, 2, 1))[..., None],
        precision=highest,
    )
    own_clean = device_clean
    before_clean = jnp.float32(1.0)
    after_clean = jnp.float32(1.0)
    carried = head_totals
    fwd_gates = []
    rev_totals = []
    rev_gates = []
    upper_list = []
    for level_bit in range(seq_bits):
        upper_half = (seq_index // 2**level_bit % 2).astype(jnp.float32)
        upper_list.append(upper_half)
        payload = (carried, own_clean)
        received = from_partner((payload[0], payload[1]), "seq", level_bit)
        far_heads = received[0]
        far_clean = received[len(received) - 1]
        rev_totals.append((1.0 - upper_half) * far_heads[0])
        rev_gates.append((1.0 - upper_half) * after_clean)
        fwd_gates.append(upper_half * before_clean)
        carried = upper_half * (far_heads[1:] + far_clean * carried[1:]) + (1.0 - upper_half) * (
            carried[1:] + own_clean * far_heads[1:]
        )
        before_clean = upper_half * far_clean * before_clean + (1.0 - upper_half) * before_clean
        after_clean = (1.0 - upper_half) * far_clean * after_clean + upper_half * after_clean
        own_clean = own_clean * far_clean
    all_tail, all_clean = (
        lax.all_gather(tail_total[None], "seq", axis=0, tiled=True),
        lax.all_gather(device_clean[None], "seq", axis=0, tiled=True),
    )
    zero_count = jnp.cumsum(1.0 - all_clean)
    device_ids = jnp.arange(seq_count)
    weight_rows = []
    for level_bit in range(seq_bits):
        stride = 2**level_bit
        block_base = (seq_index // stride ^ 1) * stride
        block_end = block_base + stride - 1
        end_count = jnp.sum(jnp.where(device_ids == block_end, zero_count, 0.0))
        inside = (
            (device_ids >= block_base) & (device_ids <= block_end) & (end_count - zero_count == 0.0)
        )
        weight_rows.append(jnp.where(inside, 1.0, 0.0) * upper_list[level_bit])
    fwd_state = jnp.einsum("km,mhnp->khnp", jnp.stack(weight_rows), all_tail, precision=highest)
    rev_state = jnp.stack(rev_totals)
    fwd_gate = jnp.stack(fwd_gates)
    rev_gate = jnp.stack(rev_gates)
    query_gate = fwd_gate[:, None, None] * query_weight[None]
    lam_query = cross_level * query_gate
    weighted_cot = cot_heads[None] * jnp.transpose(lam_query, (0, 2, 1))[..., None]
    grad_c_cross = jnp.einsum("kthp,khnp->tn", weighted_cot, fwd_state, precision=highest)
    projected = jnp.einsum("tn,khnp->kthp", c_proj, fwd_state, precision=highest)
    grad_lam_cross = query_gate * jnp.transpose(
        jnp.sum(projected * cot_heads[None], axis=-1), (0, 2, 1)
    )
    rev_combined = jnp.einsum("k,khnp->hnp", rev_gate, rev_state, precision=highest)
    key_rows = key_weight.T[:, :, None]
    grad_x_cross = jnp.einsum("sn,hnp->shp", b_proj, rev_combined, precision=highest) * key_rows
    grad_b_cross = jnp.einsum("shp,hnp->sn", x_heads * key_rows, rev_combined, precision=highest)
    local_stretch = jnp.arange(rows_dev) // STRETCH
    differ = local_stretch[:, None] ^ local_stretch[None, :]
    local_level = jnp.zeros_like(differ)
    for level_bit in range(stretch_bits):
        local_level = local_level + (differ >= 2**level_bit).astype(jnp.int32)
    local_doc = jnp.cumsum(starts)[local_stretch]
    row_ids = jnp.arange(rows_dev)
    valid = (row_ids[:, None] >= row_ids[None, :]) & (local_doc[:, None] == local_doc[None, :])
    scores = jnp.dot(c_proj, b_proj.T, precision=highest)

    def head_step(mixed_sum, pieces):
        x_one, cot_one, query_decay, key_decay, lam_one = pieces
        decayed = jnp.where(valid, query_decay[:, None] * key_decay[None, :], 0.0)
        lam_pair = jnp.zeros((rows_dev, rows_dev), jnp.float32)
        for level in range(stretch_bits + 1):
            lam_pair = jnp.where(local_level == level, lam_one[level][:, None], lam_pair)
        inner = jnp.dot(cot_one, x_one.T, precision=highest)
        kernel = decayed * lam_pair
        weighted = kernel * scores
        plain = decayed * scores * inner
        grad_x_one = jnp.dot(weighted.T, cot_one, precision=highest)
        grad_lam_one = jnp.stack(
            [
                jnp.sum(jnp.where(local_level == level, plain, 0.0), axis=1)
                for level in range(stretch_bits + 1)
            ]
        )
        return (mixed_sum + kernel * inner, (grad_x_one, grad_lam_one))

    pieces = (
        jnp.transpose(x_heads, (1, 0, 2)),
        jnp.transpose(cot_heads, (1, 0, 2)),
        decay_query,
        decay_key,
        jnp.transpose(level_vals[: stretch_bits + 1], (1, 0, 2)),
    )
    mixed_total, (grad_x_local, grad_lam_local) = lax.scan(
        head_step, jnp.zeros((rows_dev, rows_dev), jnp.float32), pieces
    )
    local_c = grad_c_cross + jnp.dot(mixed_total, b_proj, precision=highest)
    local_b = grad_b_cross + jnp.dot(mixed_total.T, c_proj, precision=highest)
    grad_x = (jnp.transpose(grad_x_local, (1, 0, 2)) + grad_x_cross).reshape(
        rows_dev, head_count * width
    )
    grad_level = (
        jnp.concatenate([jnp.transpose(grad_lam_local, (1, 0, 2)), grad_lam_cross], 0)
        * level_scale[:, None, None]
    )
    grad_b, grad_c = (
        lax.psum_scatter(local_b, "head", scatter_dimension=0, tiled=True),
        lax.psum_scatter(local_c, "head", scatter_dimension=0, tiled=True),
    )
    return (grad_x, grad_b, grad_c, grad_level)


def solution(mesh):
    return jax.shard_map(
        local,
        mesh=mesh,
        in_specs=(
            P("seq", "head"),
            P("seq", "head"),
            P("seq", None),
            P("seq", None),
            P("head"),
            P(None, "head", "seq"),
            P("seq"),
        ),
        out_specs=(
            P("seq", "head"),
            P(("seq", "head"), None),
            P(("seq", "head"), None),
            P(None, "head", "seq"),
        ),
        check_vma=False,
    )
```

profile of v0, /device:TPU:0, one launch (start us, length us, event | category | flops | bytes accessed | tf_op | source)
XLA Modules:
  0.0 729.3 jit_solution(16242255150893106869)
XLA Ops:
  13.5 6.4 fusion.61
  25.5 21.2 %all-reduce = f32[8]{0:T(128)S(1)} all-reduce(f32[8]{0:T(128)S(1)} %bitcast_dynamic-update-slice_fusion), channel_id=2, replica_groups=mesh['seq'=8,'head'=4] {'seq'}, use_global_device_ids=true, to_apply=%add | all-reduce | flops 8 | bytes 64
  47.0 5.4 copy.54
  62.4 33.9 %all-gather.4.cloned.1.call-done = f32[128,128,64]{1,2,0:T(8,128)} async-done(((f32[16,128,64]{1,2,0:T(8,128)}), f32[128,128,64]{1,2,0:T(8,128)}) %all-gather.4.cloned.1.call-update) | async-done | bytes 4194320 | tf_op jit(solution)/shard_map/all_gather | solution.py:78
  96.4 8.2 %fusion.38 = f32[3,16,128,64]{2,0,3,1:T(4,128)S(1)} fusion(f32[8,16,128,64]{2,3,1,0:T(8,128)} %bitcast.211, f32[1,8]{1,0:T(1,128)S(1)} %get-tuple-element.309, f32[1,8]{1,0:T(1,128)S(1)} %get-tuple-element.310, f32[1,8]{1,0:T(1,128)S(1)} %get-tuple-element.308), kind=kOutput, calls=%fused_computation.60 | convolution fusion | flops 37748784 | bytes 5767264 | tf_op jit(solution)/shard_map/km,mhnp->khnp/dot_general | solution.py:93
  104.6 11.6 %fusion.30 = f32[3,1024,16]{1,2,0:T(8,128)S(1)} fusion(f32[1024,16,64]{0,2,1:T(8,128)S(1)} %bitcast.202, f32[3,16,128,64]{2,0,3,1:T(4,128)S(1)} %fusion.38, f32[1024,128]{1,0:T(8,128)S(1)} %copy-done.5), kind=kOutput, calls=%fused_computation.50 | convolution fusion | flops 4838080512 | bytes 6488064 | tf_op jit(solution)/shard_map/tn,khnp->kthp/dot_general | solution.py:101
  118.0 11.2 %fusion.50 = f32[3,16,128,64]{2,3,1,0:T(8,128)} fusion(f32[3,1024,16]{1,2,0:T(8,128)S(1)} %get-tuple-element.287, f32[1024,16,64]{0,2,1:T(8,128)S(1)} %bitcast.203, f32[1024,128]{1,0:T(8,128)S(1)} %copy-done.5), kind=kOutput, calls=%fused_computation.73 | convolution fusion | flops 4834983936 | bytes 6488064 | tf_op jit(solution)/shard_map/tn,kthp->khnp/dot_general | solution.py:47
  135.2 5.4 add_select_fusion
  147.3 17.1 %collective-permute-done.2 = f32[3,16,128,64]{2,3,1,0:T(8,128)} collective-permute-done((f32[3,16,128,64]{2,3,1,0:T(8,128)}, f32[3,16,128,64]{2,3,1,0:T(8,128)}, u32[]{:S(2)}, u32[]{:S(2)}) %collective-permute-start.2) | collective-permute-done | bytes 1572896 | tf_op jit(solution)/shard_map/ppermute | solution.py:10
  169.6 465.9 %while.16 = (s32[]{:T(128)}, f32[1024,1024]{0,1:T(8,128)}, f32[16,1024,64]{1,2,0:T(8,128)}, f32[16,5,1024]{2,0,1:T(8,128)}, f32[16,1024]{1,0:T(8,128)}, /*index=...) while((s32[]{:T(128)}, f32[1024,1024]{0,1:T(8,128)}, ...), condition=%wide.region_7.8_spmd.clone.clone, body=%wide.region_1.0_spmd.clone.clone.sunk | while | flops 1703930880 | bytes 43289372 | solution.py:145
  171.4 11.7 %multiply_multiply_fusion.4 = (f32[1024,1024]{0,1:T(8,128)S(1)}, f32[1024,1024]{0,1:T(8,128)}) fusion(f32[1024,1024]{0,1:T(8,128)} %get-tuple-element.459, s32[1024]{0:T(1024)S(1)} %get-tuple-element.460, f32[1024]{0:T(1024)S(1)} %bitcast.219, f32[1024]{0:T(1024)S(1)} %bitcast.221, f32[1024]{0:T(1024)S(1)} %bitcast.231, f32[1024]{0:T(1024)S(1)} %bitcast.225, ...), kind=kOutput, calls=%fused_computation.14.clone.1 | convolution fusion | flops 839909376 | bytes 17348096 | tf_op jit(solution)/shard_map/while/body/eval_jaxpr/dot_general | solution.py:125
  183.1 9.5 %fusion.106 = f32[16,1024,64]{1,2,0:T(8,128)} fusion(f32[16,1024,64]{1,2,0:T(8,128)} %get-tuple-element.434, s32[]{:T(128)S(6)} %copy.113, f32[1024,1024]{0,1:T(8,128)S(1)} %copy-done.6, f32[1024]{0:T(1024)S(1)} %bitcast.232, f32[1024]{0:T(1024)S(1)} %bitcast.226, f32[1024]{0:T(1024)S(1)} %bitcast.228, f32[1024]{0:T(1024)S(1)} %bitcast.230, ...), kind=kOutput, calls=%fused_computation.26.clone.1 | convolution fusion | flops 835715072 | bytes 4764672 | tf_op jit(solution)/shard_map/while/body/eval_jaxpr/dot_general | solution.py:129
  200.1 12.1 %multiply_multiply_fusion.4 = (f32[1024,1024]{0,1:T(8,128)S(1)}, f32[1024,1024]{0,1:T(8,128)}) fusion(f32[1024,1024]{0,1:T(8,128)} %get-tuple-element.459, s32[1024]{0:T(1024)S(1)} %get-tuple-element.460, f32[1024]{0:T(1024)S(1)} %bitcast.219, f32[1024]{0:T(1024)S(1)} %bitcast.221, f32[1024]{0:T(1024)S(1)} %bitcast.231, f32[1024]{0:T(1024)S(1)} %bitcast.225, ...), kind=kOutput, calls=%fused_computation.14.clone.1 | convolution fusion | flops 839909376 | bytes 17348096 | tf_op jit(solution)/shard_map/while/body/eval_jaxpr/dot_general | solution.py:125
  212.2 9.5 %fusion.106 = f32[16,1024,64]{1,2,0:T(8,128)} fusion(f32[16,1024,64]{1,2,0:T(8,128)} %get-tuple-element.434, s32[]{:T(128)S(6)} %copy.113, f32[1024,1024]{0,1:T(8,128)S(1)} %copy-done.6, f32[1024]{0:T(1024)S(1)} %bitcast.232, f32[1024]{0:T(1024)S(1)} %bitcast.226, f32[1024]{0:T(1024)S(1)} %bitcast.228, f32[1024]{0:T(1024)S(1)} %bitcast.230, ...), kind=kOutput, calls=%fused_computation.26.clone.1 | convolution fusion | flops 835715072 | bytes 4764672 | tf_op jit(solution)/shard_map/while/body/eval_jaxpr/dot_general | solution.py:129
  229.2 12.1 %multiply_multiply_fusion.4 = (f32[1024,1024]{0,1:T(8,128)S(1)}, f32[1024,1024]{0,1:T(8,128)}) fusion(f32[1024,1024]{0,1:T(8,128)} %get-tuple-element.459, s32[1024]{0:T(1024)S(1)} %get-tuple-element.460, f32[1024]{0:T(1024)S(1)} %bitcast.219, f32[1024]{0:T(1024)S(1)} %bitcast.221, f32[1024]{0:T(1024)S(1)} %bitcast.231, f32[1024]{0:T(1024)S(1)} %bitcast.225, ...), kind=kOutput, calls=%fused_computation.14.clone.1 | convolution fusion | flops 839909376 | bytes 17348096 | tf_op jit(solution)/shard_map/while/body/eval_jaxpr/dot_general | solution.py:125
  241.4 9.5 %fusion.106 = f32[16,1024,64]{1,2,0:T(8,128)} fusion(f32[16,1024,64]{1,2,0:T(8,128)} %get-tuple-element.434, s32[]{:T(128)S(6)} %copy.113, f32[1024,1024]{0,1:T(8,128)S(1)} %copy-done.6, f32[1024]{0:T(1024)S(1)} %bitcast.232, f32[1024]{0:T(1024)S(1)} %bitcast.226, f32[1024]{0:T(1024)S(1)} %bitcast.228, f32[1024]{0:T(1024)S(1)} %bitcast.230, ...), kind=kOutput, calls=%fused_computation.26.clone.1 | convolution fusion | flops 835715072 | bytes 4764672 | tf_op jit(solution)/shard_map/while/body/eval_jaxpr/dot_general | solution.py:129
  258.3 12.1 %multiply_multiply_fusion.4 = (f32[1024,1024]{0,1:T(8,128)S(1)}, f32[1024,1024]{0,1:T(8,128)}) fusion(f32[1024,1024]{0,1:T(8,128)} %get-tuple-element.459, s32[1024]{0:T(1024)S(1)} %get-tuple-element.460, f32[1024]{0:T(1024)S(1)} %bitcast.219, f32[1024]{0:T(1024)S(1)} %bitcast.221, f32[1024]{0:T(1024)S(1)} %bitcast.231, f32[1024]{0:T(1024)S(1)} %bitcast.225, ...), kind=kOutput, calls=%fused_computation.14.clone.1 | convolution fusion | flops 839909376 | bytes 17348096 | tf_op jit(solution)/shard_map/while/body/eval_jaxpr/dot_general | solution.py:125
  270.5 9.5 %fusion.106 = f32[16,1024,64]{1,2,0:T(8,128)} fusion(f32[16,1024,64]{1,2,0:T(8,128)} %get-tuple-element.434, s32[]{:T(128)S(6)} %copy.113, f32[1024,1024]{0,1:T(8,128)S(1)} %copy-done.6, f32[1024]{0:T(1024)S(1)} %bitcast.232, f32[1024]{0:T(1024)S(1)} %bitcast.226, f32[1024]{0:T(1024)S(1)} %bitcast.228, f32[1024]{0:T(1024)S(1)} %bitcast.230, ...), kind=kOutput, calls=%fused_computation.26.clone.1 | convolution fusion | flops 835715072 | bytes 4764672 | tf_op jit(solution)/shard_map/while/body/eval_jaxpr/dot_general | solution.py:129
  287.5 12.1 %multiply_multiply_fusion.4 = (f32[1024,1024]{0,1:T(8,128)S(1)}, f32[1024,1024]{0,1:T(8,128)}) fusion(f32[1024,1024]{0,1:T(8,128)} %get-tuple-element.459, s32[1024]{0:T(1024)S(1)} %get-tuple-element.460, f32[1024]{0:T(1024)S(1)} %bitcast.219, f32[1024]{0:T(1024)S(1)} %bitcast.221, f32[1024]{0:T(1024)S(1)} %bitcast.231, f32[1024]{0:T(1024)S(1)} %bitcast.225, ...), kind=kOutput, calls=%fused_computation.14.clone.1 | convolution fusion | flops 839909376 | bytes 17348096 | tf_op jit(solution)/shard_map/while/body/eval_jaxpr/dot_general | solution.py:125
  299.6 9.5 %fusion.106 = f32[16,1024,64]{1,2,0:T(8,128)} fusion(f32[16,1024,64]{1,2,0:T(8,128)} %get-tuple-element.434, s32[]{:T(128)S(6)} %copy.113, f32[1024,1024]{0,1:T(8,128)S(1)} %copy-done.6, f32[1024]{0:T(1024)S(1)} %bitcast.232, f32[1024]{0:T(1024)S(1)} %bitcast.226, f32[1024]{0:T(1024)S(1)} %bitcast.228, f32[1024]{0:T(1024)S(1)} %bitcast.230, ...), kind=kOutput, calls=%fused_computation.26.clone.1 | convolution fusion | flops 835715072 | bytes 4764672 | tf_op jit(solution)/shard_map/while/body/eval_jaxpr/dot_general | solution.py:129
  316.6 12.1 %multiply_multiply_fusion.4 = (f32[1024,1024]{0,1:T(8,128)S(1)}, f32[1024,1024]{0,1:T(8,128)}) fusion(f32[1024,1024]{0,1:T(8,128)} %get-tuple-element.459, s32[1024]{0:T(1024)S(1)} %get-tuple-element.460, f32[1024]{0:T(1024)S(1)} %bitcast.219, f32[1024]{0:T(1024)S(1)} %bitcast.221, f32[1024]{0:T(1024)S(1)} %bitcast.231, f32[1024]{0:T(1024)S(1)} %bitcast.225, ...), kind=kOutput, calls=%fused_computation.14.clone.1 | convolution fusion | flops 839909376 | bytes 17348096 | tf_op jit(solution)/shard_map/while/body/eval_jaxpr/dot_general | solution.py:125
  328.7 9.5 %fusion.106 = f32[16,1024,64]{1,2,0:T(8,128)} fusion(f32[16,1024,64]{1,2,0:T(8,128)} %get-tuple-element.434, s32[]{:T(128)S(6)} %copy.113, f32[1024,1024]{0,1:T(8,128)S(1)} %copy-done.6, f32[1024]{0:T(1024)S(1)} %bitcast.232, f32[1024]{0:T(1024)S(1)} %bitcast.226, f32[1024]{0:T(1024)S(1)} %bitcast.228, f32[1024]{0:T(1024)S(1)} %bitcast.230, ...), kind=kOutput, calls=%fused_computation.26.clone.1 | convolution fusion | flops 835715072 | bytes 4764672 | tf_op jit(solution)/shard_map/while/body/eval_jaxpr/dot_general | solution.py:129
  345.7 12.1 %multiply_multiply_fusion.4 = (f32[1024,1024]{0,1:T(8,128)S(1)}, f32[1024,1024]{0,1:T(8,128)}) fusion(f32[1024,1024]{0,1:T(8,128)} %get-tuple-element.459, s32[1024]{0:T(1024)S(1)} %get-tuple-element.460, f32[1024]{0:T(1024)S(1)} %bitcast.219, f32[1024]{0:T(1024)S(1)} %bitcast.221, f32[1024]{0:T(1024)S(1)} %bitcast.231, f32[1024]{0:T(1024)S(1)} %bitcast.225, ...), kind=kOutput, calls=%fused_computation.14.clone.1 | convolution fusion | flops 839909376 | bytes 17348096 | tf_op jit(solution)/shard_map/while/body/eval_jaxpr/dot_general | solution.py:125
  357.8 9.5 %fusion.106 = f32[16,1024,64]{1,2,0:T(8,128)} fusion(f32[16,1024,64]{1,2,0:T(8,128)} %get-tuple-element.434, s32[]{:T(128)S(6)} %copy.113, f32[1024,1024]{0,1:T(8,128)S(1)} %copy-done.6, f32[1024]{0:T(1024)S(1)} %bitcast.232, f32[1024]{0:T(1024)S(1)} %bitcast.226, f32[1024]{0:T(1024)S(1)} %bitcast.228, f32[1024]{0:T(1024)S(1)} %bitcast.230, ...), kind=kOutput, calls=%fused_computation.26.clone.1 | convolution fusion | flops 835715072 | bytes 4764672 | tf_op jit(solution)/shard_map/while/body/eval_jaxpr/dot_general | solution.py:129
  374.8 12.1 %multiply_multiply_fusion.4 = (f32[1024,1024]{0,1:T(8,128)S(1)}, f32[1024,1024]{0,1:T(8,128)}) fusion(f32[1024,1024]{0,1:T(8,128)} %get-tuple-element.459, s32[1024]{0:T(1024)S(1)} %get-tuple-element.460, f32[1024]{0:T(1024)S(1)} %bitcast.219, f32[1024]{0:T(1024)S(1)} %bitcast.221, f32[1024]{0:T(1024)S(1)} %bitcast.231, f32[1024]{0:T(1024)S(1)} %bitcast.225, ...), kind=kOutput, calls=%fused_computation.14.clone.1 | convolution fusion | flops 839909376 | bytes 17348096 | tf_op jit(solution)/shard_map/while/body/eval_jaxpr/dot_general | solution.py:125
  386.9 9.5 %fusion.106 = f32[16,1024,64]{1,2,0:T(8,128)} fusion(f32[16,1024,64]{1,2,0:T(8,128)} %get-tuple-element.434, s32[]{:T(128)S(6)} %copy.113, f32[1024,1024]{0,1:T(8,128)S(1)} %copy-done.6, f32[1024]{0:T(1024)S(1)} %bitcast.232, f32[1024]{0:T(1024)S(1)} %bitcast.226, f32[1024]{0:T(1024)S(1)} %bitcast.228, f32[1024]{0:T(1024)S(1)} %bitcast.230, ...), kind=kOutput, calls=%fused_computation.26.clone.1 | convolution fusion | flops 835715072 | bytes 4764672 | tf_op jit(solution)/shard_map/while/body/eval_jaxpr/dot_general | solution.py:129
  403.9 12.1 %multiply_multiply_fusion.4 = (f32[1024,1024]{0,1:T(8,128)S(1)}, f32[1024,1024]{0,1:T(8,128)}) fusion(f32[1024,1024]{0,1:T(8,128)} %get-tuple-element.459, s32[1024]{0:T(1024)S(1)} %get-tuple-element.460, f32[1024]{0:T(1024)S(1)} %bitcast.219, f32[1024]{0:T(1024)S(1)} %bitcast.221, f32[1024]{0:T(1024)S(1)} %bitcast.231, f32[1024]{0:T(1024)S(1)} %bitcast.225, ...), kind=kOutput, calls=%fused_computation.14.clone.1 | convolution fusion | flops 839909376 | bytes 17348096 | tf_op jit(solution)/shard_map/while/body/eval_jaxpr/dot_general | solution.py:125
  416.1 9.5 %fusion.106 = f32[16,1024,64]{1,2,0:T(8,128)} fusion(f32[16,1024,64]{1,2,0:T(8,128)} %get-tuple-element.434, s32[]{:T(128)S(6)} %copy.113, f32[1024,1024]{0,1:T(8,128)S(1)} %copy-done.6, f32[1024]{0:T(1024)S(1)} %bitcast.232, f32[1024]{0:T(1024)S(1)} %bitcast.226, f32[1024]{0:T(1024)S(1)} %bitcast.228, f32[1024]{0:T(1024)S(1)} %bitcast.230, ...), kind=kOutput, calls=%fused_computation.26.clone.1 | convolution fusion | flops 835715072 | bytes 4764672 | tf_op jit(solution)/shard_map/while/body/eval_jaxpr/dot_general | solution.py:129
  433.0 12.1 %multiply_multiply_fusion.4 = (f32[1024,1024]{0,1:T(8,128)S(1)}, f32[1024,1024]{0,1:T(8,128)}) fusion(f32[1024,1024]{0,1:T(8,128)} %get-tuple-element.459, s32[1024]{0:T(1024)S(1)} %get-tuple-element.460, f32[1024]{0:T(1024)S(1)} %bitcast.219, f32[1024]{0:T(1024)S(1)} %bitcast.221, f32[1024]{0:T(1024)S(1)} %bitcast.231, f32[1024]{0:T(1024)S(1)} %bitcast.225, ...), kind=kOutput, calls=%fused_computation.14.clone.1 | convolution fusion | flops 839909376 | bytes 17348096 | tf_op jit(solution)/shard_map/while/body/eval_jaxpr/dot_general | solution.py:125
  445.2 9.5 %fusion.106 = f32[16,1024,64]{1,2,0:T(8,128)} fusion(f32[16,1024,64]{1,2,0:T(8,128)} %get-tuple-element.434, s32[]{:T(128)S(6)} %copy.113, f32[1024,1024]{0,1:T(8,128)S(1)} %copy-done.6, f32[1024]{0:T(1024)S(1)} %bitcast.232, f32[1024]{0:T(1024)S(1)} %bitcast.226, f32[1024]{0:T(1024)S(1)} %bitcast.228, f32[1024]{0:T(1024)S(1)} %bitcast.230, ...), kind=kOutput, calls=%fused_computation.26.clone.1 | convolution fusion | flops 835715072 | bytes 4764672 | tf_op jit(solution)/shard_map/while/body/eval_jaxpr/dot_general | solution.py:129
  462.1 12.1 %multiply_multiply_fusion.4 = (f32[1024,1024]{0,1:T(8,128)S(1)}, f32[1024,1024]{0,1:T(8,128)}) fusion(f32[1024,1024]{0,1:T(8,128)} %get-tuple-element.459, s32[1024]{0:T(1024)S(1)} %get-tuple-element.460, f32[1024]{0:T(1024)S(1)} %bitcast.219, f32[1024]{0:T(1024)S(1)} %bitcast.221, f32[1024]{0:T(1024)S(1)} %bitcast.231, f32[1024]{0:T(1024)S(1)} %bitcast.225, ...), kind=kOutput, calls=%fused_computation.14.clone.1 | convolution fusion | flops 839909376 | bytes 17348096 | tf_op jit(solution)/shard_map/while/body/eval_jaxpr/dot_general | solution.py:125
  474.3 9.5 %fusion.106 = f32[16,1024,64]{1,2,0:T(8,128)} fusion(f32[16,1024,64]{1,2,0:T(8,128)} %get-tuple-element.434, s32[]{:T(128)S(6)} %copy.113, f32[1024,1024]{0,1:T(8,128)S(1)} %copy-done.6, f32[1024]{0:T(1024)S(1)} %bitcast.232, f32[1024]{0:T(1024)S(1)} %bitcast.226, f32[1024]{0:T(1024)S(1)} %bitcast.228, f32[1024]{0:T(1024)S(1)} %bitcast.230, ...), kind=kOutput, calls=%fused_computation.26.clone.1 | convolution fusion | flops 835715072 | bytes 4764672 | tf_op jit(solution)/shard_map/while/body/eval_jaxpr/dot_general | solution.py:129
  491.2 12.1 %multiply_multiply_fusion.4 = (f32[1024,1024]{0,1:T(8,128)S(1)}, f32[1024,1024]{0,1:T(8,128)}) fusion(f32[1024,1024]{0,1:T(8,128)} %get-tuple-element.459, s32[1024]{0:T(1024)S(1)} %get-tuple-element.460, f32[1024]{0:T(1024)S(1)} %bitcast.219, f32[1024]{0:T(1024)S(1)} %bitcast.221, f32[1024]{0:T(1024)S(1)} %bitcast.231, f32[1024]{0:T(1024)S(1)} %bitcast.225, ...), kind=kOutput, calls=%fused_computation.14.clone.1 | convolution fusion | flops 839909376 | bytes 17348096 | tf_op jit(solution)/shard_map/while/body/eval_jaxpr/dot_general | solution.py:125
  503.4 9.4 %fusion.106 = f32[16,1024,64]{1,2,0:T(8,128)} fusion(f32[16,1024,64]{1,2,0:T(8,128)} %get-tuple-element.434, s32[]{:T(128)S(6)} %copy.113, f32[1024,1024]{0,1:T(8,128)S(1)} %copy-done.6, f32[1024]{0:T(1024)S(1)} %bitcast.232, f32[1024]{0:T(1024)S(1)} %bitcast.226, f32[1024]{0:T(1024)S(1)} %bitcast.228, f32[1024]{0:T(1024)S(1)} %bitcast.230, ...), kind=kOutput, calls=%fused_computation.26.clone.1 | convolution fusion | flops 835715072 | bytes 4764672 | tf_op jit(solution)/shard_map/while/body/eval_jaxpr/dot_general | solution.py:129
  520.3 12.1 %multiply_multiply_fusion.4 = (f32[1024,1024]{0,1:T(8,128)S(1)}, f32[1024,1024]{0,1:T(8,128)}) fusion(f32[1024,1024]{0,1:T(8,128)} %get-tuple-element.459, s32[1024]{0:T(1024)S(1)} %get-tuple-element.460, f32[1024]{0:T(1024)S(1)} %bitcast.219, f32[1024]{0:T(1024)S(1)} %bitcast.221, f32[1024]{0:T(1024)S(1)} %bitcast.231, f32[1024]{0:T(1024)S(1)} %bitcast.225, ...), kind=kOutput, calls=%fused_computation.14.clone.1 | convolution fusion | flops 839909376 | bytes 17348096 | tf_op jit(solution)/shard_map/while/body/eval_jaxpr/dot_general | solution.py:125
  532.5 9.4 %fusion.106 = f32[16,1024,64]{1,2,0:T(8,128)} fusion(f32[16,1024,64]{1,2,0:T(8,128)} %get-tuple-element.434, s32[]{:T(128)S(6)} %copy.113, f32[1024,1024]{0,1:T(8,128)S(1)} %copy-done.6, f32[1024]{0:T(1024)S(1)} %bitcast.232, f32[1024]{0:T(1024)S(1)} %bitcast.226, f32[1024]{0:T(1024)S(1)} %bitcast.228, f32[1024]{0:T(1024)S(1)} %bitcast.230, ...), kind=kOutput, calls=%fused_computation.26.clone.1 | convolution fusion | flops 835715072 | bytes 4764672 | tf_op jit(solution)/shard_map/while/body/eval_jaxpr/dot_general | solution.py:129
  549.4 12.1 %multiply_multiply_fusion.4 = (f32[1024,1024]{0,1:T(8,128)S(1)}, f32[1024,1024]{0,1:T(8,128)}) fusion(f32[1024,1024]{0,1:T(8,128)} %get-tuple-element.459, s32[1024]{0:T(1024)S(1)} %get-tuple-element.460, f32[1024]{0:T(1024)S(1)} %bitcast.219, f32[1024]{0:T(1024)S(1)} %bitcast.221, f32[1024]{0:T(1024)S(1)} %bitcast.231, f32[1024]{0:T(1024)S(1)} %bitcast.225, ...), kind=kOutput, calls=%fused_computation.14.clone.1 | convolution fusion | flops 839909376 | bytes 17348096 | tf_op jit(solution)/shard_map/while/body/eval_jaxpr/dot_general | solution.py:125
  561.6 9.4 %fusion.106 = f32[16,1024,64]{1,2,0:T(8,128)} fusion(f32[16,1024,64]{1,2,0:T(8,128)} %get-tuple-element.434, s32[]{:T(128)S(6)} %copy.113, f32[1024,1024]{0,1:T(8,128)S(1)} %copy-done.6, f32[1024]{0:T(1024)S(1)} %bitcast.232, f32[1024]{0:T(1024)S(1)} %bitcast.226, f32[1024]{0:T(1024)S(1)} %bitcast.228, f32[1024]{0:T(1024)S(1)} %bitcast.230, ...), kind=kOutput, calls=%fused_computation.26.clone.1 | convolution fusion | flops 835715072 | bytes 4764672 | tf_op jit(solution)/shard_map/while/body/eval_jaxpr/dot_general | solution.py:129
  578.5 12.1 %multiply_multiply_fusion.4 = (f32[1024,1024]{0,1:T(8,128)S(1)}, f32[1024,1024]{0,1:T(8,128)}) fusion(f32[1024,1024]{0,1:T(8,128)} %get-tuple-element.459, s32[1024]{0:T(1024)S(1)} %get-tuple-element.460, f32[1024]{0:T(1024)S(1)} %bitcast.219, f32[1024]{0:T(1024)S(1)} %bitcast.221, f32[1024]{0:T(1024)S(1)} %bitcast.231, f32[1024]{0:T(1024)S(1)} %bitcast.225, ...), kind=kOutput, calls=%fused_computation.14.clone.1 | convolution fusion | flops 839909376 | bytes 17348096 | tf_op jit(solution)/shard_map/while/body/eval_jaxpr/dot_general | solution.py:125
  590.7 9.4 %fusion.106 = f32[16,1024,64]{1,2,0:T(8,128)} fusion(f32[16,1024,64]{1,2,0:T(8,128)} %get-tuple-element.434, s32[]{:T(128)S(6)} %copy.113, f32[1024,1024]{0,1:T(8,128)S(1)} %copy-done.6, f32[1024]{0:T(1024)S(1)} %bitcast.232, f32[1024]{0:T(1024)S(1)} %bitcast.226, f32[1024]{0:T(1024)S(1)} %bitcast.228, f32[1024]{0:T(1024)S(1)} %bitcast.230, ...), kind=kOutput, calls=%fused_computation.26.clone.1 | convolution fusion | flops 835715072 | bytes 4764672 | tf_op jit(solution)/shard_map/while/body/eval_jaxpr/dot_general | solution.py:129
  607.6 12.1 %multiply_multiply_fusion.4 = (f32[1024,1024]{0,1:T(8,128)S(1)}, f32[1024,1024]{0,1:T(8,128)}) fusion(f32[1024,1024]{0,1:T(8,128)} %get-tuple-element.459, s32[1024]{0:T(1024)S(1)} %get-tuple-element.460, f32[1024]{0:T(1024)S(1)} %bitcast.219, f32[1024]{0:T(1024)S(1)} %bitcast.221, f32[1024]{0:T(1024)S(1)} %bitcast.231, f32[1024]{0:T(1024)S(1)} %bitcast.225, ...), kind=kOutput, calls=%fused_computation.14.clone.1 | convolution fusion | flops 839909376 | bytes 17348096 | tf_op jit(solution)/shard_map/while/body/eval_jaxpr/dot_general | solution.py:125
  619.7 9.5 %fusion.106 = f32[16,1024,64]{1,2,0:T(8,128)} fusion(f32[16,1024,64]{1,2,0:T(8,128)} %get-tuple-element.434, s32[]{:T(128)S(6)} %copy.113, f32[1024,1024]{0,1:T(8,128)S(1)} %copy-done.6, f32[1024]{0:T(1024)S(1)} %bitcast.232, f32[1024]{0:T(1024)S(1)} %bitcast.226, f32[1024]{0:T(1024)S(1)} %bitcast.228, f32[1024]{0:T(1024)S(1)} %bitcast.230, ...), kind=kOutput, calls=%fused_computation.26.clone.1 | convolution fusion | flops 835715072 | bytes 4764672 | tf_op jit(solution)/shard_map/while/body/eval_jaxpr/dot_general | solution.py:129
  636.8 22.2 %fusion.53 = f32[1024,128]{1,0:T(8,128)S(1)} fusion(f32[3,16,128,64]{2,0,3,1:T(4,128)S(1)} %fusion.38, f32[3,1024,16]{1,2,0:T(8,128)} %get-tuple-element.286, f32[1024,16,64]{0,2,1:T(8,128)} %bitcast.204), kind=kOutput, calls=%fused_computation.74 | convolution fusion | flops 4834983936 | bytes 6488064 | tf_op jit(solution)/shard_map/kthp,khnp->tn/dot_general | solution.py:100
  663.7 7.7 %convolution_add_fusion = f32[1024,128]{1,0:T(8,128)} fusion(f32[1024,128]{1,0:T(8,128)S(1)} %fusion.53, f32[1024,1024]{0,1:T(8,128)S(1)} %copy-done.3, f32[1024,128]{1,0:T(8,128)S(1)} %copy-done), kind=kOutput, calls=%fused_computation.75 | convolution fusion | flops 1610743808 | bytes 5767168 | tf_op jit(solution)/shard_map/dot_general | solution.py:148
  672.7 12.9 %collective-permute-done.4 = f32[1,16,128,64]{2,3,1,0:T(8,128)S(1)} collective-permute-done((f32[1,16,128,64]{2,3,1,0:T(8,128)S(1)}, f32[1,16,128,64]{2,3,1,0:T(8,128)S(1)}, u32[]{:S(2)}, u32[]{:S(2)}) %collective-permute-start.4) | collective-permute-done | bytes 524320 | tf_op jit(solution)/shard_map/ppermute | solution.py:10
  690.4 6.7 fusion.58
  702.3 6.7 fusion.37
  714.4 8.2 %reduce-scatter.3.cloned.1.call-done = f32[256,128]{1,0:T(8,128)} async-done(((f32[1024,128]{1,0:T(8,128)}), f32[256,128]{1,0:T(8,128)}) %reduce-scatter.3.cloned.1.call-update) | async-done | bytes 131088 | tf_op jit(solution)/shard_map/reduce_scatter | solution.py:158
  (225 shorter events, 179.9 us)
Async XLA Ops:
  7.2 6.3 copy-start
  7.2 89.2 %all-gather.4.cloned.1.call-start = ((), (), s32[]{:S(2)}) async-start(), calls=%async_computation.4 | async-start | bytes 4718592 | tf_op jit(solution)/shard_map/all_gather | solution.py:78
  7.2 5.4 copy-start.10
  7.3 6.1 copy-start.9
  12.7 7.9 %copy-start.11 = (u32[32]{0:T(128)S(1)}, u32[32]{0:T(128)}, u32[]{:S(2)}) copy-start(u32[32]{0:T(128)} %constant.177) | copy-start | bytes 388
  19.9 694.5 %reduce-scatter.5.cloned.1.call-start = ((), (), s32[]{:S(2)}) async-start(), calls=%async_computation.3 | async-start | bytes 655360 | tf_op jit(solution)/shard_map/reduce_scatter | solution.py:159
  22.5 34.3 %collective-permute-start = (f32[]{:T(128)}, f32[]{:T(128)}, u32[]{:S(2)}, u32[]{:S(2)}) collective-permute-start(f32[]{:T(128)} %bitcast.26), channel_id=1, source_target_pairs={{0,4},{4,0},{8,12},{12,8},{16,20},{20,16},{24,28},{28,24},{1,5},{5... | collective-permute-start | bytes 20 | tf_op jit(solution)/shard_map/ppermute | solution.py:10
  47.0 8.9 %copy-start.7 = (f32[8,16,1024]{2,1,0:T(8,128)S(1)}, f32[8,16,1024]{2,1,0:T(8,128)}, u32[]{:S(2)}) copy-start(f32[8,16,1024]{2,1,0:T(8,128)} %param.14) | copy-start | bytes 1572868
  52.4 52.2 %copy-start.5 = (f32[1024,128]{1,0:T(8,128)S(1)}, f32[1024,128]{1,0:T(8,128)}, u32[]{:S(2)}) copy-start(f32[1024,128]{1,0:T(8,128)} %param.12) | copy-start | bytes 1572868
  58.1 3.6 collective-permute-start.1
  96.3 8.3 %copy-start.1 = (f32[1024,1024]{0,1:T(8,128)S(1)}, f32[1024,1024]{0,1:T(8,128)}, u32[]{:S(2)}) copy-start(f32[1024,1024]{0,1:T(8,128)} %copy.54) | copy-start | bytes 12582916
  129.2 35.3 %collective-permute-start.2 = (f32[3,16,128,64]{2,3,1,0:T(8,128)}, f32[3,16,128,64]{2,3,1,0:T(8,128)}, u32[]{:S(2)}, u32[]{:S(2)}) collective-permute-start(f32[3,16,128,64]{2,3,1,0:T(8,128)} %fusion.50), channel_id=1, source_target_pairs={{0,4},{4,0},{8,12},{12,8},{16,20},{20,16},{24,28},{28,24},{1,5},{5... | collective-permute-start | bytes 4718600 | tf_op jit(solution)/shard_map/ppermute | solution.py:10
  168.6 490.4 %collective-permute-start.3 = (f32[2,16,128,64]{2,3,1,0:T(8,128)}, f32[2,16,128,64]{2,3,1,0:T(8,128)}, u32[]{:S(2)}, u32[]{:S(2)}) collective-permute-start(f32[2,16,128,64]{2,3,1,0:T(8,128)} %multiply_add_fusion), channel_id=1, source_target_pairs={{0,8},{4,12},{8,0},{12,4},{16,24},{20,28},{24,16},{28,20},{1,9},{5... | collective-permute-start | bytes 3145736 | tf_op jit(solution)/shard_map/ppermute | solution.py:10
  171.4 11.7 %copy-start.6 = (f32[1024,1024]{0,1:T(8,128)S(1)}, f32[1024,1024]{0,1:T(8,128)}, u32[]{:S(2)}) copy-start(f32[1024,1024]{0,1:T(8,128)} %get-tuple-element.459) | copy-start | bytes 12582916 | tf_op jit(solution)/shard_map/while
  200.1 12.1 %copy-start.6 = (f32[1024,1024]{0,1:T(8,128)S(1)}, f32[1024,1024]{0,1:T(8,128)}, u32[]{:S(2)}) copy-start(f32[1024,1024]{0,1:T(8,128)} %get-tuple-element.459) | copy-start | bytes 12582916 | tf_op jit(solution)/shard_map/while
  229.2 12.1 %copy-start.6 = (f32[1024,1024]{0,1:T(8,128)S(1)}, f32[1024,1024]{0,1:T(8,128)}, u32[]{:S(2)}) copy-start(f32[1024,1024]{0,1:T(8,128)} %get-tuple-element.459) | copy-start | bytes 12582916 | tf_op jit(solution)/shard_map/while
  258.3 12.1 %copy-start.6 = (f32[1024,1024]{0,1:T(8,128)S(1)}, f32[1024,1024]{0,1:T(8,128)}, u32[]{:S(2)}) copy-start(f32[1024,1024]{0,1:T(8,128)} %get-tuple-element.459) | copy-start | bytes 12582916 | tf_op jit(solution)/shard_map/while
  287.5 12.1 %copy-start.6 = (f32[1024,1024]{0,1:T(8,128)S(1)}, f32[1024,1024]{0,1:T(8,128)}, u32[]{:S(2)}) copy-start(f32[1024,1024]{0,1:T(8,128)} %get-tuple-element.459) | copy-start | bytes 12582916 | tf_op jit(solution)/shard_map/while
  316.6 12.1 %copy-start.6 = (f32[1024,1024]{0,1:T(8,128)S(1)}, f32[1024,1024]{0,1:T(8,128)}, u32[]{:S(2)}) copy-start(f32[1024,1024]{0,1:T(8,128)} %get-tuple-element.459) | copy-start | bytes 12582916 | tf_op jit(solution)/shard_map/while
  345.7 12.1 %copy-start.6 = (f32[1024,1024]{0,1:T(8,128)S(1)}, f32[1024,1024]{0,1:T(8,128)}, u32[]{:S(2)}) copy-start(f32[1024,1024]{0,1:T(8,128)} %get-tuple-element.459) | copy-start | bytes 12582916 | tf_op jit(solution)/shard_map/while
  374.8 12.1 %copy-start.6 = (f32[1024,1024]{0,1:T(8,128)S(1)}, f32[1024,1024]{0,1:T(8,128)}, u32[]{:S(2)}) copy-start(f32[1024,1024]{0,1:T(8,128)} %get-tuple-element.459) | copy-start | bytes 12582916 | tf_op jit(solution)/shard_map/while
  403.9 12.1 %copy-start.6 = (f32[1024,1024]{0,1:T(8,128)S(1)}, f32[1024,1024]{0,1:T(8,128)}, u32[]{:S(2)}) copy-start(f32[1024,1024]{0,1:T(8,128)} %get-tuple-element.459) | copy-start | bytes 12582916 | tf_op jit(solution)/shard_map/while
  433.0 12.1 %copy-start.6 = (f32[1024,1024]{0,1:T(8,128)S(1)}, f32[1024,1024]{0,1:T(8,128)}, u32[]{:S(2)}) copy-start(f32[1024,1024]{0,1:T(8,128)} %get-tuple-element.459) | copy-start | bytes 12582916 | tf_op jit(solution)/shard_map/while
  462.1 12.1 %copy-start.6 = (f32[1024,1024]{0,1:T(8,128)S(1)}, f32[1024,1024]{0,1:T(8,128)}, u32[]{:S(2)}) copy-start(f32[1024,1024]{0,1:T(8,128)} %get-tuple-element.459) | copy-start | bytes 12582916 | tf_op jit(solution)/shard_map/while
  491.2 12.1 %copy-start.6 = (f32[1024,1024]{0,1:T(8,128)S(1)}, f32[1024,1024]{0,1:T(8,128)}, u32[]{:S(2)}) copy-start(f32[1024,1024]{0,1:T(8,128)} %get-tuple-element.459) | copy-start | bytes 12582916 | tf_op jit(solution)/shard_map/while
  520.3 12.1 %copy-start.6 = (f32[1024,1024]{0,1:T(8,128)S(1)}, f32[1024,1024]{0,1:T(8,128)}, u32[]{:S(2)}) copy-start(f32[1024,1024]{0,1:T(8,128)} %get-tuple-element.459) | copy-start | bytes 12582916 | tf_op jit(solution)/shard_map/while
  549.4 12.1 %copy-start.6 = (f32[1024,1024]{0,1:T(8,128)S(1)}, f32[1024,1024]{0,1:T(8,128)}, u32[]{:S(2)}) copy-start(f32[1024,1024]{0,1:T(8,128)} %get-tuple-element.459) | copy-start | bytes 12582916 | tf_op jit(solution)/shard_map/while
  578.5 12.1 %copy-start.6 = (f32[1024,1024]{0,1:T(8,128)S(1)}, f32[1024,1024]{0,1:T(8,128)}, u32[]{:S(2)}) copy-start(f32[1024,1024]{0,1:T(8,128)} %get-tuple-element.459) | copy-start | bytes 12582916 | tf_op jit(solution)/shard_map/while
  607.6 12.1 %copy-start.6 = (f32[1024,1024]{0,1:T(8,128)S(1)}, f32[1024,1024]{0,1:T(8,128)}, u32[]{:S(2)}) copy-start(f32[1024,1024]{0,1:T(8,128)} %get-tuple-element.459) | copy-start | bytes 12582916 | tf_op jit(solution)/shard_map/while
  636.8 26.9 %copy-start.3 = (f32[1024,1024]{0,1:T(8,128)S(1)}, f32[1024,1024]{0,1:T(8,128)}, u32[]{:S(2)}) copy-start(f32[1024,1024]{0,1:T(8,128)} %get-tuple-element.96) | copy-start | bytes 12582916
  661.2 24.5 %collective-permute-start.4 = (f32[1,16,128,64]{2,3,1,0:T(8,128)S(1)}, f32[1,16,128,64]{2,3,1,0:T(8,128)S(1)}, u32[]{:S(2)}, u32[]{:S(2)}) collective-permute-start(f32[1,16,128,64]{2,3,1,0:T(8,128)S(1)} %get-tuple-element.285), channel_id=1, source_target_pairs={{0,16},{4,20},{8,24},{12,28},{16,0},{20,4},{24,8},{28,12},{1,17},{... | collective-permute-start | bytes 1572872 | tf_op jit(solution)/shard_map/ppermute | solution.py:10
  671.4 51.1 %reduce-scatter.3.cloned.1.call-start = ((), (), s32[]{:S(2)}) async-start(), calls=%async_computation.2 | async-start | bytes 655360 | tf_op jit(solution)/shard_map/reduce_scatter | solution.py:158
  671.5 18.9 %copy-start.2 = (f32[16,1024,64]{1,2,0:T(8,128)S(1)}, f32[16,1024,64]{1,2,0:T(8,128)}, u32[]{:S(2)}) copy-start(f32[16,1024,64]{1,2,0:T(8,128)} %get-tuple-element.472) | copy-start | bytes 12582916
  685.8 11.3 %copy-start.4 = (f32[1024,1024]{0,1:T(8,128)S(1)}, f32[1024,1024]{0,1:T(8,128)}, u32[]{:S(2)}) copy-start(f32[1024,1024]{0,1:T(8,128)} %get-tuple-element.96) | copy-start | bytes 12582916
  697.1 4.3 copy-start.8
Sparse Core Ops, SparseCore 0:
  20.0 76.3 all-gather.3
  671.5 19.2 reduce-scatter.4
  701.5 20.9 reduce-scatter.2
where the time goes:
time: 737 us; the launch traced here: 729 us
  matrix products  440 us (60%)
  other arithmetic  91.3 us (12%)
  local copies, waits for them, and re-layouts  75.5 us (10%)
  waiting for transfers between devices  73.7 us (10%)
  blocking collectives  21.2 us (3%)
  between operations  18.3 us (2%)
  starting transfers between devices  8.59 us (1%)
    dot_general x16, matrix products, head_step(): inner = jnp.dot(cot_one, x_one.T, precision=highest)  194 us
    dot_general x16, matrix products, head_step(): grad_x_one = jnp.dot(weighted.T, cot_one, precision=highest)  151 us
    reduce_sum x16, other arithmetic, head_step(): jnp.sum(jnp.where(local_level == level, plain, 0.0), axis=1)  66 us
    all_gather x1, waiting for transfers between devices, local(): lax.all_gather(tail_total[None], 'seq', axis=0, tiled=True)  33.9 us
    ppermute x5, waiting for transfers between devices, from_partner(): lax.ppermute(x, axis, [(i, i ^ 1 << apart) for i in range(lax.axis_size(a...  31.6 us
    dynamic_update_slice x32, local copies, waits for them, and re-layouts, local(): lax.scan(head_step, jnp.zeros((rows_dev, rows_dev), jnp.float32), pieces)  26.7 us
    dot_general x1, matrix products, local(): jnp.einsum('kthp,khnp->tn', weighted_cot, fwd_state, precision=highest)  22.2 us
    unnamed x1, blocking collectives  21.2 us
  transfers between devices with their start and end apart: 8, of which 5 were waited for; matrix products, arithmetic and copies ran while one was open for 76% of the time, Pallas kernels for 0%

commit v1 on v0

--- a/solution.py
+++ b/solution.py
@@ -4,6 +4,28 @@
 from jax.sharding import PartitionSpec as P
 
 STRETCH = 64
+
+
+def in_order(blocks, dim):
+    blocks = jnp.moveaxis(blocks, 0, dim)
+    shape = blocks.shape
+    return blocks.reshape(*shape[:dim], shape[dim] * shape[dim + 1], *shape[dim + 2 :])
+
+
+def collect(x, axis, dim):
+    size = lax.axis_size(axis)
+    pairs = [(i, (i + 1) % size) for i in range(size)]
+    back = [(b, a) for a, b in pairs]
+    lower, upper = ([], [])
+    for lap in range(size - 1):
+        if lap % 2 == 0:
+            lower.append(lax.ppermute(lower[-1] if lower else x, axis, pairs))
+        else:
+            upper.append(lax.ppermute(upper[-1] if upper else x, axis, back))
+    parts = jnp.stack([*lower[::-1], x, *upper])
+    shift = lax.axis_index(axis) - len(lower)
+    parts = parts[(jnp.arange(size) - shift) % size]
+    return in_order(parts, dim)
 
 
 def from_partner(x, axis, apart):
@@ -75,7 +97,7 @@
         after_clean = (1.0 - upper_half) * far_clean * after_clean + upper_half * after_clean
         own_clean = own_clean * far_clean
     all_tail, all_clean = (
-        lax.all_gather(tail_total[None], "seq", axis=0, tiled=True),
+        collect(tail_total[None], "seq", 0),
         lax.all_gather(device_clean[None], "seq", axis=0, tiled=True),
     )
     zero_count = jnp.cumsum(1.0 - all_clean)

time: 737 us -> 766 us (1.039)
  local copies, waits for them, and re-layouts: 75.5 us -> 89.1 us
  starting transfers between devices: 8.59 us -> 21.1 us
    ppermute x0 -> x7, waiting for transfers between devices: none -> 34.8 us  [the longest x4 31.3 us: collect(): lower.append(lax.ppermute(lower[-1] if lower else x, axis, pairs))]
    all_gather x1 -> x0, waiting for transfers between devices: 33.9 us -> none  [local(): lax.all_gather(tail_total[None], 'seq', axis=0, tiled=True)]
    ppermute x0 -> x7, starting transfers between devices: none -> 18.2 us  [the longest x3 10 us: collect(): upper.append(lax.ppermute(upper[-1] if upper else x, axis, back))]
    unnamed x28 -> x33, local copies, waits for them, and re-layouts: 18.1 us -> 25.9 us
  transfers between devices with their start and end apart: 8 -> 14, of which waited for: 5 -> 7; matrix products, arithmetic and copies ran while one was open for 76% -> 74% of each run, Pallas kernels for 0% -> 0%
where the time goes in v1:
time: 766 us; the launch traced here: 758 us
  matrix products  439 us (57%)
  other arithmetic  92.4 us (12%)
  local copies, waits for them, and re-layouts  89.1 us (12%)
  waiting for transfers between devices  74.8 us (10%)
  blocking collectives  22.4 us (3%)
  starting transfers between devices  21.1 us (3%)
  between operations  18.6 us (2%)
    dot_general x16, matrix products, head_step(): inner = jnp.dot(cot_one, x_one.T, precision=highest)  194 us
    dot_general x16, matrix products, head_step(): grad_x_one = jnp.dot(weighted.T, cot_one, precision=highest)  151 us
    reduce_sum x16, other arithmetic, head_step(): jnp.sum(jnp.where(local_level == level, plain, 0.0), axis=1)  66 us
    ppermute x5, waiting for transfers between devices, from_partner(): lax.ppermute(x, axis, [(i, i ^ 1 << apart) for i in range(lax.axis_size(a...  33.2 us
    ppermute x4, waiting for transfers between devices, collect(): lower.append(lax.ppermute(lower[-1] if lower else x, axis, pairs))  31.3 us
    dynamic_update_slice x32, local copies, waits for them, and re-layouts, local(): lax.scan(head_step, jnp.zeros((rows_dev, rows_dev), jnp.float32), pieces)  26.7 us
    unnamed x33, local copies, waits for them, and re-layouts  25.9 us
    unnamed x1, blocking collectives  22.4 us
  transfers between devices with their start and end apart: 14, of which 7 were waited for; matrix products, arithmetic and copies ran while one was open for 74% of the time, Pallas kernels for 0%

profile of v1, /device:TPU:0, one launch (start us, length us, event | category | flops | bytes accessed | tf_op | source)
XLA Modules:
  0.0 758.1 jit_solution(6514457014831514184)
XLA Ops:
  13.5 5.4 fusion.40
  25.0 19.3 %collective-permute-done.5 = f32[1,16,128,64]{2,3,1,0:T(8,128)S(1)} collective-permute-done((f32[1,16,128,64]{2,3,1,0:T(8,128)S(1)}, f32[1,16,128,64]{2,3,1,0:T(8,128)S(1)}, u32[]{:S(2)}, u32[]{:S(2)}) %collective-permute-start.5) | collective-permute-done | bytes 524320 | tf_op jit(solution)/shard_map/ppermute | solution.py:22
  49.9 22.4 %all-reduce = f32[8]{0:T(128)S(1)} all-reduce(f32[8]{0:T(128)S(1)} %bitcast_dynamic-update-slice_fusion.8), channel_id=2, replica_groups=mesh['seq'=8,'head'=4] {'seq'}, use_global_device_ids=true, to_apply=%add | all-reduce | flops 8 | bytes 64
  80.9 12.0 %collective-permute-done.7 = f32[1,16,128,64]{2,3,1,0:T(8,128)S(1)} collective-permute-done((f32[1,16,128,64]{2,3,1,0:T(8,128)S(1)}, f32[1,16,128,64]{2,3,1,0:T(8,128)S(1)}, u32[]{:S(2)}, u32[]{:S(2)}) %collective-permute-start.7) | collective-permute-done | bytes 524320 | tf_op jit(solution)/shard_map/ppermute | solution.py:22
  127.9 8.2 %fusion.38 = f32[3,16,128,64]{2,0,3,1:T(4,128)S(1)} fusion(f32[8,16,128,64]{2,3,1,0:T(8,128)} %gather_fusion, f32[1,8]{1,0:T(1,128)S(1)} %get-tuple-element.277, f32[1,8]{1,0:T(1,128)S(1)} %get-tuple-element.278, f32[1,8]{1,0:T(1,128)S(1)} %get-tuple-element.276), kind=kOutput, calls=%fused_computation.61 | convolution fusion | flops 37748784 | bytes 5767264 | tf_op jit(solution)/shard_map/km,mhnp->khnp/dot_general | solution.py:115
  136.2 11.6 %fusion.30 = f32[3,1024,16]{1,2,0:T(8,128)S(1)} fusion(f32[1024,16,64]{0,2,1:T(8,128)S(1)} %bitcast.222, f32[3,16,128,64]{2,0,3,1:T(4,128)S(1)} %fusion.38, f32[1024,128]{1,0:T(8,128)S(1)} %copy-done.5), kind=kOutput, calls=%fused_computation.51 | convolution fusion | flops 4838080512 | bytes 6488064 | tf_op jit(solution)/shard_map/tn,khnp->kthp/dot_general | solution.py:123
  149.6 11.2 %fusion.50 = f32[3,16,128,64]{2,3,1,0:T(8,128)} fusion(f32[3,1024,16]{1,2,0:T(8,128)S(1)} %get-tuple-element.255, f32[1024,16,64]{0,2,1:T(8,128)S(1)} %bitcast.223, f32[1024,128]{1,0:T(8,128)S(1)} %copy-done.5), kind=kOutput, calls=%fused_computation.74 | convolution fusion | flops 4834983936 | bytes 6488064 | tf_op jit(solution)/shard_map/tn,kthp->khnp/dot_general | solution.py:69
  166.6 5.4 add_select_fusion
  178.7 17.4 %collective-permute-done.2 = f32[3,16,128,64]{2,3,1,0:T(8,128)} collective-permute-done((f32[3,16,128,64]{2,3,1,0:T(8,128)}, f32[3,16,128,64]{2,3,1,0:T(8,128)}, u32[]{:S(2)}, u32[]{:S(2)}) %collective-permute-start.2) | collective-permute-done | bytes 1572896 | tf_op jit(solution)/shard_map/ppermute | solution.py:32
  200.2 465.9 %while.16 = (s32[]{:T(128)}, f32[1024,1024]{0,1:T(8,128)}, f32[16,1024,64]{1,2,0:T(8,128)}, f32[16,5,1024]{2,0,1:T(8,128)}, f32[16,1024]{1,0:T(8,128)}, /*index=...) while((s32[]{:T(128)}, f32[1024,1024]{0,1:T(8,128)}, ...), condition=%wide.region_7.8_spmd.clone.clone, body=%wide.region_1.7_spmd.clone.clone.sunk | while | flops 1703930880 | bytes 43289372 | solution.py:167
  202.1 11.7 %multiply_multiply_fusion.4 = (f32[1024,1024]{0,1:T(8,128)S(1)}, f32[1024,1024]{0,1:T(8,128)}) fusion(f32[1024,1024]{0,1:T(8,128)} %get-tuple-element.427, s32[1024]{0:T(1024)S(1)} %get-tuple-element.428, f32[1024]{0:T(1024)S(1)} %bitcast.240, f32[1024]{0:T(1024)S(1)} %bitcast.242, f32[1024]{0:T(1024)S(1)} %bitcast.252, f32[1024]{0:T(1024)S(1)} %bitcast.246, ...), kind=kOutput, calls=%fused_computation.15.clone.1 | convolution fusion | flops 839909376 | bytes 17348096 | tf_op jit(solution)/shard_map/while/body/eval_jaxpr/dot_general | solution.py:147
  213.8 9.5 %fusion.105 = f32[16,1024,64]{1,2,0:T(8,128)} fusion(f32[16,1024,64]{1,2,0:T(8,128)} %get-tuple-element.402, s32[]{:T(128)S(6)} %copy.84, f32[1024,1024]{0,1:T(8,128)S(1)} %copy-done.6, f32[1024]{0:T(1024)S(1)} %bitcast.253, f32[1024]{0:T(1024)S(1)} %bitcast.247, f32[1024]{0:T(1024)S(1)} %bitcast.249, f32[1024]{0:T(1024)S(1)} %bitcast.251, ...), kind=kOutput, calls=%fused_computation.27.clone.1 | convolution fusion | flops 835715072 | bytes 4764672 | tf_op jit(solution)/shard_map/while/body/eval_jaxpr/dot_general | solution.py:151
  230.7 12.1 %multiply_multiply_fusion.4 = (f32[1024,1024]{0,1:T(8,128)S(1)}, f32[1024,1024]{0,1:T(8,128)}) fusion(f32[1024,1024]{0,1:T(8,128)} %get-tuple-element.427, s32[1024]{0:T(1024)S(1)} %get-tuple-element.428, f32[1024]{0:T(1024)S(1)} %bitcast.240, f32[1024]{0:T(1024)S(1)} %bitcast.242, f32[1024]{0:T(1024)S(1)} %bitcast.252, f32[1024]{0:T(1024)S(1)} %bitcast.246, ...), kind=kOutput, calls=%fused_computation.15.clone.1 | convolution fusion | flops 839909376 | bytes 17348096 | tf_op jit(solution)/shard_map/while/body/eval_jaxpr/dot_general | solution.py:147
  242.9 9.5 %fusion.105 = f32[16,1024,64]{1,2,0:T(8,128)} fusion(f32[16,1024,64]{1,2,0:T(8,128)} %get-tuple-element.402, s32[]{:T(128)S(6)} %copy.84, f32[1024,1024]{0,1:T(8,128)S(1)} %copy-done.6, f32[1024]{0:T(1024)S(1)} %bitcast.253, f32[1024]{0:T(1024)S(1)} %bitcast.247, f32[1024]{0:T(1024)S(1)} %bitcast.249, f32[1024]{0:T(1024)S(1)} %bitcast.251, ...), kind=kOutput, calls=%fused_computation.27.clone.1 | convolution fusion | flops 835715072 | bytes 4764672 | tf_op jit(solution)/shard_map/while/body/eval_jaxpr/dot_general | solution.py:151
  259.8 12.1 %multiply_multiply_fusion.4 = (f32[1024,1024]{0,1:T(8,128)S(1)}, f32[1024,1024]{0,1:T(8,128)}) fusion(f32[1024,1024]{0,1:T(8,128)} %get-tuple-element.427, s32[1024]{0:T(1024)S(1)} %get-tuple-element.428, f32[1024]{0:T(1024)S(1)} %bitcast.240, f32[1024]{0:T(1024)S(1)} %bitcast.242, f32[1024]{0:T(1024)S(1)} %bitcast.252, f32[1024]{0:T(1024)S(1)} %bitcast.246, ...), kind=kOutput, calls=%fused_computation.15.clone.1 | convolution fusion | flops 839909376 | bytes 17348096 | tf_op jit(solution)/shard_map/while/body/eval_jaxpr/dot_general | solution.py:147
  272.0 9.5 %fusion.105 = f32[16,1024,64]{1,2,0:T(8,128)} fusion(f32[16,1024,64]{1,2,0:T(8,128)} %get-tuple-element.402, s32[]{:T(128)S(6)} %copy.84, f32[1024,1024]{0,1:T(8,128)S(1)} %copy-done.6, f32[1024]{0:T(1024)S(1)} %bitcast.253, f32[1024]{0:T(1024)S(1)} %bitcast.247, f32[1024]{0:T(1024)S(1)} %bitcast.249, f32[1024]{0:T(1024)S(1)} %bitcast.251, ...), kind=kOutput, calls=%fused_computation.27.clone.1 | convolution fusion | flops 835715072 | bytes 4764672 | tf_op jit(solution)/shard_map/while/body/eval_jaxpr/dot_general | solution.py:151
  289.0 12.1 %multiply_multiply_fusion.4 = (f32[1024,1024]{0,1:T(8,128)S(1)}, f32[1024,1024]{0,1:T(8,128)}) fusion(f32[1024,1024]{0,1:T(8,128)} %get-tuple-element.427, s32[1024]{0:T(1024)S(1)} %get-tuple-element.428, f32[1024]{0:T(1024)S(1)} %bitcast.240, f32[1024]{0:T(1024)S(1)} %bitcast.242, f32[1024]{0:T(1024)S(1)} %bitcast.252, f32[1024]{0:T(1024)S(1)} %bitcast.246, ...), kind=kOutput, calls=%fused_computation.15.clone.1 | convolution fusion | flops 839909376 | bytes 17348096 | tf_op jit(solution)/shard_map/while/body/eval_jaxpr/dot_general | solution.py:147
  301.1 9.5 %fusion.105 = f32[16,1024,64]{1,2,0:T(8,128)} fusion(f32[16,1024,64]{1,2,0:T(8,128)} %get-tuple-element.402, s32[]{:T(128)S(6)} %copy.84, f32[1024,1024]{0,1:T(8,128)S(1)} %copy-done.6, f32[1024]{0:T(1024)S(1)} %bitcast.253, f32[1024]{0:T(1024)S(1)} %bitcast.247, f32[1024]{0:T(1024)S(1)} %bitcast.249, f32[1024]{0:T(1024)S(1)} %bitcast.251, ...), kind=kOutput, calls=%fused_computation.27.clone.1 | convolution fusion | flops 835715072 | bytes 4764672 | tf_op jit(solution)/shard_map/while/body/eval_jaxpr/dot_general | solution.py:151
  318.1 12.1 %multiply_multiply_fusion.4 = (f32[1024,1024]{0,1:T(8,128)S(1)}, f32[1024,1024]{0,1:T(8,128)}) fusion(f32[1024,1024]{0,1:T(8,128)} %get-tuple-element.427, s32[1024]{0:T(1024)S(1)} %get-tuple-element.428, f32[1024]{0:T(1024)S(1)} %bitcast.240, f32[1024]{0:T(1024)S(1)} %bitcast.242, f32[1024]{0:T(1024)S(1)} %bitcast.252, f32[1024]{0:T(1024)S(1)} %bitcast.246, ...), kind=kOutput, calls=%fused_computation.15.clone.1 | convolution fusion | flops 839909376 | bytes 17348096 | tf_op jit(solution)/shard_map/while/body/eval_jaxpr/dot_general | solution.py:147
  330.2 9.5 %fusion.105 = f32[16,1024,64]{1,2,0:T(8,128)} fusion(f32[16,1024,64]{1,2,0:T(8,128)} %get-tuple-element.402, s32[]{:T(128)S(6)} %copy.84, f32[1024,1024]{0,1:T(8,128)S(1)} %copy-done.6, f32[1024]{0:T(1024)S(1)} %bitcast.253, f32[1024]{0:T(1024)S(1)} %bitcast.247, f32[1024]{0:T(1024)S(1)} %bitcast.249, f32[1024]{0:T(1024)S(1)} %bitcast.251, ...), kind=kOutput, calls=%fused_computation.27.clone.1 | convolution fusion | flops 835715072 | bytes 4764672 | tf_op jit(solution)/shard_map/while/body/eval_jaxpr/dot_general | solution.py:151
  347.2 12.1 %multiply_multiply_fusion.4 = (f32[1024,1024]{0,1:T(8,128)S(1)}, f32[1024,1024]{0,1:T(8,128)}) fusion(f32[1024,1024]{0,1:T(8,128)} %get-tuple-element.427, s32[1024]{0:T(1024)S(1)} %get-tuple-element.428, f32[1024]{0:T(1024)S(1)} %bitcast.240, f32[1024]{0:T(1024)S(1)} %bitcast.242, f32[1024]{0:T(1024)S(1)} %bitcast.252, f32[1024]{0:T(1024)S(1)} %bitcast.246, ...), kind=kOutput, calls=%fused_computation.15.clone.1 | convolution fusion | flops 839909376 | bytes 17348096 | tf_op jit(solution)/shard_map/while/body/eval_jaxpr/dot_general | solution.py:147
  359.3 9.5 %fusion.105 = f32[16,1024,64]{1,2,0:T(8,128)} fusion(f32[16,1024,64]{1,2,0:T(8,128)} %get-tuple-element.402, s32[]{:T(128)S(6)} %copy.84, f32[1024,1024]{0,1:T(8,128)S(1)} %copy-done.6, f32[1024]{0:T(1024)S(1)} %bitcast.253, f32[1024]{0:T(1024)S(1)} %bitcast.247, f32[1024]{0:T(1024)S(1)} %bitcast.249, f32[1024]{0:T(1024)S(1)} %bitcast.251, ...), kind=kOutput, calls=%fused_computation.27.clone.1 | convolution fusion | flops 835715072 | bytes 4764672 | tf_op jit(solution)/shard_map/while/body/eval_jaxpr/dot_general | solution.py:151
  376.3 12.1 %multiply_multiply_fusion.4 = (f32[1024,1024]{0,1:T(8,128)S(1)}, f32[1024,1024]{0,1:T(8,128)}) fusion(f32[1024,1024]{0,1:T(8,128)} %get-tuple-element.427, s32[1024]{0:T(1024)S(1)} %get-tuple-element.428, f32[1024]{0:T(1024)S(1)} %bitcast.240, f32[1024]{0:T(1024)S(1)} %bitcast.242, f32[1024]{0:T(1024)S(1)} %bitcast.252, f32[1024]{0:T(1024)S(1)} %bitcast.246, ...), kind=kOutput, calls=%fused_computation.15.clone.1 | convolution fusion | flops 839909376 | bytes 17348096 | tf_op jit(solution)/shard_map/while/body/eval_jaxpr/dot_general | solution.py:147
  388.5 9.5 %fusion.105 = f32[16,1024,64]{1,2,0:T(8,128)} fusion(f32[16,1024,64]{1,2,0:T(8,128)} %get-tuple-element.402, s32[]{:T(128)S(6)} %copy.84, f32[1024,1024]{0,1:T(8,128)S(1)} %copy-done.6, f32[1024]{0:T(1024)S(1)} %bitcast.253, f32[1024]{0:T(1024)S(1)} %bitcast.247, f32[1024]{0:T(1024)S(1)} %bitcast.249, f32[1024]{0:T(1024)S(1)} %bitcast.251, ...), kind=kOutput, calls=%fused_computation.27.clone.1 | convolution fusion | flops 835715072 | bytes 4764672 | tf_op jit(solution)/shard_map/while/body/eval_jaxpr/dot_general | solution.py:151
  405.4 12.1 %multiply_multiply_fusion.4 = (f32[1024,1024]{0,1:T(8,128)S(1)}, f32[1024,1024]{0,1:T(8,128)}) fusion(f32[1024,1024]{0,1:T(8,128)} %get-tuple-element.427, s32[1024]{0:T(1024)S(1)} %get-tuple-element.428, f32[1024]{0:T(1024)S(1)} %bitcast.240, f32[1024]{0:T(1024)S(1)} %bitcast.242, f32[1024]{0:T(1024)S(1)} %bitcast.252, f32[1024]{0:T(1024)S(1)} %bitcast.246, ...), kind=kOutput, calls=%fused_computation.15.clone.1 | convolution fusion | flops 839909376 | bytes 17348096 | tf_op jit(solution)/shard_map/while/body/eval_jaxpr/dot_general | solution.py:147
  417.6 9.5 %fusion.105 = f32[16,1024,64]{1,2,0:T(8,128)} fusion(f32[16,1024,64]{1,2,0:T(8,128)} %get-tuple-element.402, s32[]{:T(128)S(6)} %copy.84, f32[1024,1024]{0,1:T(8,128)S(1)} %copy-done.6, f32[1024]{0:T(1024)S(1)} %bitcast.253, f32[1024]{0:T(1024)S(1)} %bitcast.247, f32[1024]{0:T(1024)S(1)} %bitcast.249, f32[1024]{0:T(1024)S(1)} %bitcast.251, ...), kind=kOutput, calls=%fused_computation.27.clone.1 | convolution fusion | flops 835715072 | bytes 4764672 | tf_op jit(solution)/shard_map/while/body/eval_jaxpr/dot_general | solution.py:151
  434.5 12.1 %multiply_multiply_fusion.4 = (f32[1024,1024]{0,1:T(8,128)S(1)}, f32[1024,1024]{0,1:T(8,128)}) fusion(f32[1024,1024]{0,1:T(8,128)} %get-tuple-element.427, s32[1024]{0:T(1024)S(1)} %get-tuple-element.428, f32[1024]{0:T(1024)S(1)} %bitcast.240, f32[1024]{0:T(1024)S(1)} %bitcast.242, f32[1024]{0:T(1024)S(1)} %bitcast.252, f32[1024]{0:T(1024)S(1)} %bitcast.246, ...), kind=kOutput, calls=%fused_computation.15.clone.1 | convolution fusion | flops 839909376 | bytes 17348096 | tf_op jit(solution)/shard_map/while/body/eval_jaxpr/dot_general | solution.py:147
  446.7 9.5 %fusion.105 = f32[16,1024,64]{1,2,0:T(8,128)} fusion(f32[16,1024,64]{1,2,0:T(8,128)} %get-tuple-element.402, s32[]{:T(128)S(6)} %copy.84, f32[1024,1024]{0,1:T(8,128)S(1)} %copy-done.6, f32[1024]{0:T(1024)S(1)} %bitcast.253, f32[1024]{0:T(1024)S(1)} %bitcast.247, f32[1024]{0:T(1024)S(1)} %bitcast.249, f32[1024]{0:T(1024)S(1)} %bitcast.251, ...), kind=kOutput, calls=%fused_computation.27.clone.1 | convolution fusion | flops 835715072 | bytes 4764672 | tf_op jit(solution)/shard_map/while/body/eval_jaxpr/dot_general | solution.py:151
  463.7 12.1 %multiply_multiply_fusion.4 = (f32[1024,1024]{0,1:T(8,128)S(1)}, f32[1024,1024]{0,1:T(8,128)}) fusion(f32[1024,1024]{0,1:T(8,128)} %get-tuple-element.427, s32[1024]{0:T(1024)S(1)} %get-tuple-element.428, f32[1024]{0:T(1024)S(1)} %bitcast.240, f32[1024]{0:T(1024)S(1)} %bitcast.242, f32[1024]{0:T(1024)S(1)} %bitcast.252, f32[1024]{0:T(1024)S(1)} %bitcast.246, ...), kind=kOutput, calls=%fused_computation.15.clone.1 | convolution fusion | flops 839909376 | bytes 17348096 | tf_op jit(solution)/shard_map/while/body/eval_jaxpr/dot_general | solution.py:147
  475.8 9.5 %fusion.105 = f32[16,1024,64]{1,2,0:T(8,128)} fusion(f32[16,1024,64]{1,2,0:T(8,128)} %get-tuple-element.402, s32[]{:T(128)S(6)} %copy.84, f32[1024,1024]{0,1:T(8,128)S(1)} %copy-done.6, f32[1024]{0:T(1024)S(1)} %bitcast.253, f32[1024]{0:T(1024)S(1)} %bitcast.247, f32[1024]{0:T(1024)S(1)} %bitcast.249, f32[1024]{0:T(1024)S(1)} %bitcast.251, ...), kind=kOutput, calls=%fused_computation.27.clone.1 | convolution fusion | flops 835715072 | bytes 4764672 | tf_op jit(solution)/shard_map/while/body/eval_jaxpr/dot_general | solution.py:151
  492.8 12.1 %multiply_multiply_fusion.4 = (f32[1024,1024]{0,1:T(8,128)S(1)}, f32[1024,1024]{0,1:T(8,128)}) fusion(f32[1024,1024]{0,1:T(8,128)} %get-tuple-element.427, s32[1024]{0:T(1024)S(1)} %get-tuple-element.428, f32[1024]{0:T(1024)S(1)} %bitcast.240, f32[1024]{0:T(1024)S(1)} %bitcast.242, f32[1024]{0:T(1024)S(1)} %bitcast.252, f32[1024]{0:T(1024)S(1)} %bitcast.246, ...), kind=kOutput, calls=%fused_computation.15.clone.1 | convolution fusion | flops 839909376 | bytes 17348096 | tf_op jit(solution)/shard_map/while/body/eval_jaxpr/dot_general | solution.py:147
  504.9 9.5 %fusion.105 = f32[16,1024,64]{1,2,0:T(8,128)} fusion(f32[16,1024,64]{1,2,0:T(8,128)} %get-tuple-element.402, s32[]{:T(128)S(6)} %copy.84, f32[1024,1024]{0,1:T(8,128)S(1)} %copy-done.6, f32[1024]{0:T(1024)S(1)} %bitcast.253, f32[1024]{0:T(1024)S(1)} %bitcast.247, f32[1024]{0:T(1024)S(1)} %bitcast.249, f32[1024]{0:T(1024)S(1)} %bitcast.251, ...), kind=kOutput, calls=%fused_computation.27.clone.1 | convolution fusion | flops 835715072 | bytes 4764672 | tf_op jit(solution)/shard_map/while/body/eval_jaxpr/dot_general | solution.py:151
  521.9 12.1 %multiply_multiply_fusion.4 = (f32[1024,1024]{0,1:T(8,128)S(1)}, f32[1024,1024]{0,1:T(8,128)}) fusion(f32[1024,1024]{0,1:T(8,128)} %get-tuple-element.427, s32[1024]{0:T(1024)S(1)} %get-tuple-element.428, f32[1024]{0:T(1024)S(1)} %bitcast.240, f32[1024]{0:T(1024)S(1)} %bitcast.242, f32[1024]{0:T(1024)S(1)} %bitcast.252, f32[1024]{0:T(1024)S(1)} %bitcast.246, ...), kind=kOutput, calls=%fused_computation.15.clone.1 | convolution fusion | flops 839909376 | bytes 17348096 | tf_op jit(solution)/shard_map/while/body/eval_jaxpr/dot_general | solution.py:147
  534.0 9.4 %fusion.105 = f32[16,1024,64]{1,2,0:T(8,128)} fusion(f32[16,1024,64]{1,2,0:T(8,128)} %get-tuple-element.402, s32[]{:T(128)S(6)} %copy.84, f32[1024,1024]{0,1:T(8,128)S(1)} %copy-done.6, f32[1024]{0:T(1024)S(1)} %bitcast.253, f32[1024]{0:T(1024)S(1)} %bitcast.247, f32[1024]{0:T(1024)S(1)} %bitcast.249, f32[1024]{0:T(1024)S(1)} %bitcast.251, ...), kind=kOutput, calls=%fused_computation.27.clone.1 | convolution fusion | flops 835715072 | bytes 4764672 | tf_op jit(solution)/shard_map/while/body/eval_jaxpr/dot_general | solution.py:151
  551.0 12.1 %multiply_multiply_fusion.4 = (f32[1024,1024]{0,1:T(8,128)S(1)}, f32[1024,1024]{0,1:T(8,128)}) fusion(f32[1024,1024]{0,1:T(8,128)} %get-tuple-element.427, s32[1024]{0:T(1024)S(1)} %get-tuple-element.428, f32[1024]{0:T(1024)S(1)} %bitcast.240, f32[1024]{0:T(1024)S(1)} %bitcast.242, f32[1024]{0:T(1024)S(1)} %bitcast.252, f32[1024]{0:T(1024)S(1)} %bitcast.246, ...), kind=kOutput, calls=%fused_computation.15.clone.1 | convolution fusion | flops 839909376 | bytes 17348096 | tf_op jit(solution)/shard_map/while/body/eval_jaxpr/dot_general | solution.py:147
  563.1 9.4 %fusion.105 = f32[16,1024,64]{1,2,0:T(8,128)} fusion(f32[16,1024,64]{1,2,0:T(8,128)} %get-tuple-element.402, s32[]{:T(128)S(6)} %copy.84, f32[1024,1024]{0,1:T(8,128)S(1)} %copy-done.6, f32[1024]{0:T(1024)S(1)} %bitcast.253, f32[1024]{0:T(1024)S(1)} %bitcast.247, f32[1024]{0:T(1024)S(1)} %bitcast.249, f32[1024]{0:T(1024)S(1)} %bitcast.251, ...), kind=kOutput, calls=%fused_computation.27.clone.1 | convolution fusion | flops 835715072 | bytes 4764672 | tf_op jit(solution)/shard_map/while/body/eval_jaxpr/dot_general | solution.py:151
  580.1 12.1 %multiply_multiply_fusion.4 = (f32[1024,1024]{0,1:T(8,128)S(1)}, f32[1024,1024]{0,1:T(8,128)}) fusion(f32[1024,1024]{0,1:T(8,128)} %get-tuple-element.427, s32[1024]{0:T(1024)S(1)} %get-tuple-element.428, f32[1024]{0:T(1024)S(1)} %bitcast.240, f32[1024]{0:T(1024)S(1)} %bitcast.242, f32[1024]{0:T(1024)S(1)} %bitcast.252, f32[1024]{0:T(1024)S(1)} %bitcast.246, ...), kind=kOutput, calls=%fused_computation.15.clone.1 | convolution fusion | flops 839909376 | bytes 17348096 | tf_op jit(solution)/shard_map/while/body/eval_jaxpr/dot_general | solution.py:147
  592.2 9.4 %fusion.105 = f32[16,1024,64]{1,2,0:T(8,128)} fusion(f32[16,1024,64]{1,2,0:T(8,128)} %get-tuple-element.402, s32[]{:T(128)S(6)} %copy.84, f32[1024,1024]{0,1:T(8,128)S(1)} %copy-done.6, f32[1024]{0:T(1024)S(1)} %bitcast.253, f32[1024]{0:T(1024)S(1)} %bitcast.247, f32[1024]{0:T(1024)S(1)} %bitcast.249, f32[1024]{0:T(1024)S(1)} %bitcast.251, ...), kind=kOutput, calls=%fused_computation.27.clone.1 | convolution fusion | flops 835715072 | bytes 4764672 | tf_op jit(solution)/shard_map/while/body/eval_jaxpr/dot_general | solution.py:151
  609.1 12.1 %multiply_multiply_fusion.4 = (f32[1024,1024]{0,1:T(8,128)S(1)}, f32[1024,1024]{0,1:T(8,128)}) fusion(f32[1024,1024]{0,1:T(8,128)} %get-tuple-element.427, s32[1024]{0:T(1024)S(1)} %get-tuple-element.428, f32[1024]{0:T(1024)S(1)} %bitcast.240, f32[1024]{0:T(1024)S(1)} %bitcast.242, f32[1024]{0:T(1024)S(1)} %bitcast.252, f32[1024]{0:T(1024)S(1)} %bitcast.246, ...), kind=kOutput, calls=%fused_computation.15.clone.1 | convolution fusion | flops 839909376 | bytes 17348096 | tf_op jit(solution)/shard_map/while/body/eval_jaxpr/dot_general | solution.py:147
  621.3 9.4 %fusion.105 = f32[16,1024,64]{1,2,0:T(8,128)} fusion(f32[16,1024,64]{1,2,0:T(8,128)} %get-tuple-element.402, s32[]{:T(128)S(6)} %copy.84, f32[1024,1024]{0,1:T(8,128)S(1)} %copy-done.6, f32[1024]{0:T(1024)S(1)} %bitcast.253, f32[1024]{0:T(1024)S(1)} %bitcast.247, f32[1024]{0:T(1024)S(1)} %bitcast.249, f32[1024]{0:T(1024)S(1)} %bitcast.251, ...), kind=kOutput, calls=%fused_computation.27.clone.1 | convolution fusion | flops 835715072 | bytes 4764672 | tf_op jit(solution)/shard_map/while/body/eval_jaxpr/dot_general | solution.py:151
  638.2 12.1 %multiply_multiply_fusion.4 = (f32[1024,1024]{0,1:T(8,128)S(1)}, f32[1024,1024]{0,1:T(8,128)}) fusion(f32[1024,1024]{0,1:T(8,128)} %get-tuple-element.427, s32[1024]{0:T(1024)S(1)} %get-tuple-element.428, f32[1024]{0:T(1024)S(1)} %bitcast.240, f32[1024]{0:T(1024)S(1)} %bitcast.242, f32[1024]{0:T(1024)S(1)} %bitcast.252, f32[1024]{0:T(1024)S(1)} %bitcast.246, ...), kind=kOutput, calls=%fused_computation.15.clone.1 | convolution fusion | flops 839909376 | bytes 17348096 | tf_op jit(solution)/shard_map/while/body/eval_jaxpr/dot_general | solution.py:147
  650.4 9.5 %fusion.105 = f32[16,1024,64]{1,2,0:T(8,128)} fusion(f32[16,1024,64]{1,2,0:T(8,128)} %get-tuple-element.402, s32[]{:T(128)S(6)} %copy.84, f32[1024,1024]{0,1:T(8,128)S(1)} %copy-done.6, f32[1024]{0:T(1024)S(1)} %bitcast.253, f32[1024]{0:T(1024)S(1)} %bitcast.247, f32[1024]{0:T(1024)S(1)} %bitcast.249, f32[1024]{0:T(1024)S(1)} %bitcast.251, ...), kind=kOutput, calls=%fused_computation.27.clone.1 | convolution fusion | flops 835715072 | bytes 4764672 | tf_op jit(solution)/shard_map/while/body/eval_jaxpr/dot_general | solution.py:151
  667.4 22.2 %fusion.53 = f32[1024,128]{1,0:T(8,128)S(1)} fusion(f32[3,16,128,64]{2,0,3,1:T(4,128)S(1)} %fusion.38, f32[3,1024,16]{1,2,0:T(8,128)} %get-tuple-element.254, f32[1024,16,64]{0,2,1:T(8,128)} %bitcast.224), kind=kOutput, calls=%fused_computation.75 | convolution fusion | flops 4834983936 | bytes 6488064 | tf_op jit(solution)/shard_map/kthp,khnp->tn/dot_general | solution.py:122
  692.3 7.7 %convolution_add_fusion = f32[1024,128]{1,0:T(8,128)} fusion(f32[1024,128]{1,0:T(8,128)S(1)} %fusion.53, f32[1024,1024]{0,1:T(8,128)S(1)} %copy-done.3, f32[1024,128]{1,0:T(8,128)S(1)} %copy-done), kind=kOutput, calls=%fused_computation.76 | convolution fusion | flops 1610743808 | bytes 5767168 | tf_op jit(solution)/shard_map/dot_general | solution.py:170
  701.3 14.3 %collective-permute-done.4 = f32[1,16,128,64]{2,3,1,0:T(8,128)S(1)} collective-permute-done((f32[1,16,128,64]{2,3,1,0:T(8,128)S(1)}, f32[1,16,128,64]{2,3,1,0:T(8,128)S(1)}, u32[]{:S(2)}, u32[]{:S(2)}) %collective-permute-start.4) | collective-permute-done | bytes 524320 | tf_op jit(solution)/shard_map/ppermute | solution.py:32
  720.3 6.7 fusion.58
  732.3 6.7 fusion.37
  744.3 6.8 reduce-scatter.3.cloned.1.call-done
  (245 shorter events, 215.9 us)
Async XLA Ops:
  7.2 6.3 copy-start
  7.2 737.1 %reduce-scatter.5.cloned.1.call-start = ((), (), s32[]{:S(2)}) async-start(), calls=%async_computation.3 | async-start | bytes 655360 | tf_op jit(solution)/shard_map/reduce_scatter | solution.py:181
  7.2 5.4 copy-start.9
  7.3 6.1 copy-start.8
  12.7 34.8 %copy-start.10 = (u32[32]{0:T(128)S(1)}, u32[32]{0:T(128)}, u32[]{:S(2)}) copy-start(u32[32]{0:T(128)} %constant.194) | copy-start | bytes 388
  18.9 25.4 %collective-permute-start.5 = (f32[1,16,128,64]{2,3,1,0:T(8,128)S(1)}, f32[1,16,128,64]{2,3,1,0:T(8,128)S(1)}, u32[]{:S(2)}, u32[]{:S(2)}) collective-permute-start(f32[1,16,128,64]{2,3,1,0:T(8,128)S(1)} %bitcast.232), channel_id=1, source_target_pairs={{0,4},{4,8},{8,12},{12,16},{16,20},{20,24},{24,28},{28,0},{1,5},{5... | collective-permute-start | bytes 1572872 | tf_op jit(solution)/shard_map/ppermute | solution.py:22
  21.9 54.6 %collective-permute-start.9 = (f32[1,16,128,64]{2,3,1,0:T(8,128)S(1)}, f32[1,16,128,64]{2,3,1,0:T(8,128)S(1)}, u32[]{:S(2)}, u32[]{:S(2)}) collective-permute-start(f32[1,16,128,64]{2,3,1,0:T(8,128)S(1)} %bitcast.233), channel_id=1, source_target_pairs={{4,0},{8,4},{12,8},{16,12},{20,16},{24,20},{28,24},{0,28},{5,1},{9... | collective-permute-start | bytes 1572872 | tf_op jit(solution)/shard_map/ppermute | solution.py:24
  44.3 29.2 %collective-permute-start.6 = (f32[1,16,128,64]{2,3,1,0:T(8,128)S(1)}, f32[1,16,128,64]{2,3,1,0:T(8,128)S(1)}, u32[]{:S(2)}, u32[]{:S(2)}) collective-permute-start(f32[1,16,128,64]{2,3,1,0:T(8,128)S(1)} %collective-permute-done.5), channel_id=1, source_target_pairs={{0,4},{4,8},{8,12},{12,16},{16,20},{20,24},{24,28},{28,0},{1,5},{5... | collective-permute-start | bytes 1572872 | tf_op jit(solution)/shard_map/ppermute | solution.py:22
  49.3 53.4 %collective-permute-start = (f32[]{:T(128)}, f32[]{:T(128)}, u32[]{:S(2)}, u32[]{:S(2)}) collective-permute-start(f32[]{:T(128)} %bitcast.26), channel_id=1, source_target_pairs={{0,4},{4,0},{8,12},{12,8},{16,20},{20,16},{24,28},{28,24},{1,5},{5... | collective-permute-start | bytes 20 | tf_op jit(solution)/shard_map/ppermute | solution.py:32
  73.5 19.5 %collective-permute-start.7 = (f32[1,16,128,64]{2,3,1,0:T(8,128)S(1)}, f32[1,16,128,64]{2,3,1,0:T(8,128)S(1)}, u32[]{:S(2)}, u32[]{:S(2)}) collective-permute-start(f32[1,16,128,64]{2,3,1,0:T(8,128)S(1)} %collective-permute-done.6), channel_id=1, source_target_pairs={{0,4},{4,8},{8,12},{12,16},{16,20},{20,24},{24,28},{28,0},{1,5},{5... | collective-permute-start | bytes 1572872 | tf_op jit(solution)/shard_map/ppermute | solution.py:22
  76.4 31.9 %collective-permute-start.10 = (f32[1,16,128,64]{2,3,1,0:T(8,128)S(1)}, f32[1,16,128,64]{2,3,1,0:T(8,128)}, u32[]{:S(2)}, u32[]{:S(2)}) collective-permute-start(f32[1,16,128,64]{2,3,1,0:T(8,128)S(1)} %collective-permute-done.9), channel_id=1, source_target_pairs={{4,0},{8,4},{12,8},{16,12},{20,16},{24,20},{28,24},{0,28},{5,1},{9... | collective-permute-start | bytes 1572872 | tf_op jit(solution)/shard_map/ppermute | solution.py:24
  92.9 17.8 %collective-permute-start.8 = (f32[1,16,128,64]{2,3,1,0:T(8,128)S(1)}, f32[1,16,128,64]{2,3,1,0:T(8,128)}, u32[]{:S(2)}, u32[]{:S(2)}) collective-permute-start(f32[1,16,128,64]{2,3,1,0:T(8,128)S(1)} %collective-permute-done.7), channel_id=1, source_target_pairs={{0,4},{4,8},{8,12},{12,16},{16,20},{20,24},{24,28},{28,0},{1,5},{5... | collective-permute-start | bytes 1572872 | tf_op jit(solution)/shard_map/ppermute | solution.py:22
  104.0 3.6 collective-permute-start.1
  108.3 13.8 %collective-permute-start.11 = (f32[1,16,128,64]{2,3,1,0:T(8,128)}, f32[1,16,128,64]{2,3,1,0:T(8,128)S(1)}, u32[]{:S(2)}, u32[]{:S(2)}) collective-permute-start(f32[1,16,128,64]{2,3,1,0:T(8,128)} %collective-permute-done.10), channel_id=1, source_target_pairs={{4,0},{8,4},{12,8},{16,12},{20,16},{24,20},{28,24},{0,28},{5,1},{9... | collective-permute-start | bytes 1572872 | tf_op jit(solution)/shard_map/ppermute | solution.py:24
  127.9 8.3 %copy-start.1 = (f32[1024,1024]{0,1:T(8,128)S(1)}, f32[1024,1024]{0,1:T(8,128)}, u32[]{:S(2)}) copy-start(f32[1024,1024]{0,1:T(8,128)} %copy.25) | copy-start | bytes 12582916
  127.9 8.3 %copy-start.5 = (f32[1024,128]{1,0:T(8,128)S(1)}, f32[1024,128]{1,0:T(8,128)}, u32[]{:S(2)}) copy-start(f32[1024,128]{1,0:T(8,128)} %param.12) | copy-start | bytes 1572868
  160.8 35.3 %collective-permute-start.2 = (f32[3,16,128,64]{2,3,1,0:T(8,128)}, f32[3,16,128,64]{2,3,1,0:T(8,128)}, u32[]{:S(2)}, u32[]{:S(2)}) collective-permute-start(f32[3,16,128,64]{2,3,1,0:T(8,128)} %fusion.50), channel_id=1, source_target_pairs={{0,4},{4,0},{8,12},{12,8},{16,20},{20,16},{24,28},{28,24},{1,5},{5... | collective-permute-start | bytes 4718600 | tf_op jit(solution)/shard_map/ppermute | solution.py:32
  200.2 489.4 %collective-permute-start.3 = (f32[2,16,128,64]{2,3,1,0:T(8,128)}, f32[2,16,128,64]{2,3,1,0:T(8,128)}, u32[]{:S(2)}, u32[]{:S(2)}) collective-permute-start(f32[2,16,128,64]{2,3,1,0:T(8,128)} %multiply_add_fusion), channel_id=1, source_target_pairs={{0,8},{4,12},{8,0},{12,4},{16,24},{20,28},{24,16},{28,20},{1,9},{5... | collective-permute-start | bytes 3145736 | tf_op jit(solution)/shard_map/ppermute | solution.py:32
  202.0 11.7 %copy-start.6 = (f32[1024,1024]{0,1:T(8,128)S(1)}, f32[1024,1024]{0,1:T(8,128)}, u32[]{:S(2)}) copy-start(f32[1024,1024]{0,1:T(8,128)} %get-tuple-element.427) | copy-start | bytes 12582916 | tf_op jit(solution)/shard_map/while
  230.7 12.1 %copy-start.6 = (f32[1024,1024]{0,1:T(8,128)S(1)}, f32[1024,1024]{0,1:T(8,128)}, u32[]{:S(2)}) copy-start(f32[1024,1024]{0,1:T(8,128)} %get-tuple-element.427) | copy-start | bytes 12582916 | tf_op jit(solution)/shard_map/while
  259.8 12.1 %copy-start.6 = (f32[1024,1024]{0,1:T(8,128)S(1)}, f32[1024,1024]{0,1:T(8,128)}, u32[]{:S(2)}) copy-start(f32[1024,1024]{0,1:T(8,128)} %get-tuple-element.427) | copy-start | bytes 12582916 | tf_op jit(solution)/shard_map/while
  289.0 12.1 %copy-start.6 = (f32[1024,1024]{0,1:T(8,128)S(1)}, f32[1024,1024]{0,1:T(8,128)}, u32[]{:S(2)}) copy-start(f32[1024,1024]{0,1:T(8,128)} %get-tuple-element.427) | copy-start | bytes 12582916 | tf_op jit(solution)/shard_map/while
  318.1 12.1 %copy-start.6 = (f32[1024,1024]{0,1:T(8,128)S(1)}, f32[1024,1024]{0,1:T(8,128)}, u32[]{:S(2)}) copy-start(f32[1024,1024]{0,1:T(8,128)} %get-tuple-element.427) | copy-start | bytes 12582916 | tf_op jit(solution)/shard_map/while
  347.2 12.1 %copy-start.6 = (f32[1024,1024]{0,1:T(8,128)S(1)}, f32[1024,1024]{0,1:T(8,128)}, u32[]{:S(2)}) copy-start(f32[1024,1024]{0,1:T(8,128)} %get-tuple-element.427) | copy-start | bytes 12582916 | tf_op jit(solution)/shard_map/while
  376.3 12.1 %copy-start.6 = (f32[1024,1024]{0,1:T(8,128)S(1)}, f32[1024,1024]{0,1:T(8,128)}, u32[]{:S(2)}) copy-start(f32[1024,1024]{0,1:T(8,128)} %get-tuple-element.427) | copy-start | bytes 12582916 | tf_op jit(solution)/shard_map/while
  405.4 12.1 %copy-start.6 = (f32[1024,1024]{0,1:T(8,128)S(1)}, f32[1024,1024]{0,1:T(8,128)}, u32[]{:S(2)}) copy-start(f32[1024,1024]{0,1:T(8,128)} %get-tuple-element.427) | copy-start | bytes 12582916 | tf_op jit(solution)/shard_map/while
  434.5 12.1 %copy-start.6 = (f32[1024,1024]{0,1:T(8,128)S(1)}, f32[1024,1024]{0,1:T(8,128)}, u32[]{:S(2)}) copy-start(f32[1024,1024]{0,1:T(8,128)} %get-tuple-element.427) | copy-start | bytes 12582916 | tf_op jit(solution)/shard_map/while
  463.6 12.1 %copy-start.6 = (f32[1024,1024]{0,1:T(8,128)S(1)}, f32[1024,1024]{0,1:T(8,128)}, u32[]{:S(2)}) copy-start(f32[1024,1024]{0,1:T(8,128)} %get-tuple-element.427) | copy-start | bytes 12582916 | tf_op jit(solution)/shard_map/while
  492.8 12.1 %copy-start.6 = (f32[1024,1024]{0,1:T(8,128)S(1)}, f32[1024,1024]{0,1:T(8,128)}, u32[]{:S(2)}) copy-start(f32[1024,1024]{0,1:T(8,128)} %get-tuple-element.427) | copy-start | bytes 12582916 | tf_op jit(solution)/shard_map/while
  521.9 12.1 %copy-start.6 = (f32[1024,1024]{0,1:T(8,128)S(1)}, f32[1024,1024]{0,1:T(8,128)}, u32[]{:S(2)}) copy-start(f32[1024,1024]{0,1:T(8,128)} %get-tuple-element.427) | copy-start | bytes 12582916 | tf_op jit(solution)/shard_map/while
  551.0 12.1 %copy-start.6 = (f32[1024,1024]{0,1:T(8,128)S(1)}, f32[1024,1024]{0,1:T(8,128)}, u32[]{:S(2)}) copy-start(f32[1024,1024]{0,1:T(8,128)} %get-tuple-element.427) | copy-start | bytes 12582916 | tf_op jit(solution)/shard_map/while
  580.1 12.1 %copy-start.6 = (f32[1024,1024]{0,1:T(8,128)S(1)}, f32[1024,1024]{0,1:T(8,128)}, u32[]{:S(2)}) copy-start(f32[1024,1024]{0,1:T(8,128)} %get-tuple-element.427) | copy-start | bytes 12582916 | tf_op jit(solution)/shard_map/while
  609.1 12.1 %copy-start.6 = (f32[1024,1024]{0,1:T(8,128)S(1)}, f32[1024,1024]{0,1:T(8,128)}, u32[]{:S(2)}) copy-start(f32[1024,1024]{0,1:T(8,128)} %get-tuple-element.427) | copy-start | bytes 12582916 | tf_op jit(solution)/shard_map/while
  638.2 12.1 %copy-start.6 = (f32[1024,1024]{0,1:T(8,128)S(1)}, f32[1024,1024]{0,1:T(8,128)}, u32[]{:S(2)}) copy-start(f32[1024,1024]{0,1:T(8,128)} %get-tuple-element.427) | copy-start | bytes 12582916 | tf_op jit(solution)/shard_map/while
  667.4 24.9 %copy-start.3 = (f32[1024,1024]{0,1:T(8,128)S(1)}, f32[1024,1024]{0,1:T(8,128)}, u32[]{:S(2)}) copy-start(f32[1024,1024]{0,1:T(8,128)} %get-tuple-element.96) | copy-start | bytes 12582916
  691.8 23.8 %collective-permute-start.4 = (f32[1,16,128,64]{2,3,1,0:T(8,128)S(1)}, f32[1,16,128,64]{2,3,1,0:T(8,128)S(1)}, u32[]{:S(2)}, u32[]{:S(2)}) collective-permute-start(f32[1,16,128,64]{2,3,1,0:T(8,128)S(1)} %get-tuple-element.253), channel_id=1, source_target_pairs={{0,16},{4,20},{8,24},{12,28},{16,0},{20,4},{24,8},{28,12},{1,17},{... | collective-permute-start | bytes 1572872 | tf_op jit(solution)/shard_map/ppermute | solution.py:32
  700.0 51.1 %reduce-scatter.3.cloned.1.call-start = ((), (), s32[]{:S(2)}) async-start(), calls=%async_computation.2 | async-start | bytes 655360 | tf_op jit(solution)/shard_map/reduce_scatter | solution.py:180
  700.0 20.3 %copy-start.2 = (f32[16,1024,64]{1,2,0:T(8,128)S(1)}, f32[16,1024,64]{1,2,0:T(8,128)}, u32[]{:S(2)}) copy-start(f32[16,1024,64]{1,2,0:T(8,128)} %get-tuple-element.439) | copy-start | bytes 12582916
  715.8 11.3 %copy-start.4 = (f32[1024,1024]{0,1:T(8,128)S(1)}, f32[1024,1024]{0,1:T(8,128)}, u32[]{:S(2)}) copy-start(f32[1024,1024]{0,1:T(8,128)} %get-tuple-element.96) | copy-start | bytes 12582916
  727.1 4.3 copy-start.7
Sparse Core Ops, SparseCore 0:
  700.1 22.3 reduce-scatter.4
  731.5 19.5 reduce-scatter.2
